TPU v7x, 256 devices: a whole 4x4x8 slice. The times are simulated.
256 devices in a mesh: rows: 64 (over x, y_lo, z), cols: 4 (over y_hi, core).
Axes of the slice: x: 4, y: 4 (y_hi: 2, y_lo: 2; y = y_hi * 2 + y_lo), z: 8, core: 2. Of those that a mesh axis runs over, the one named last changes fastest.
Arguments:
- right_side: float32 [32, 131072], P(None, ('rows', 'cols')), may hold values from -6 to 6
- local_inverse: float32 [64, 4, 1024, 1024], P('rows', 'cols'), may hold values from -1 to 2.5, as said below
- modes: float32 [64, 4, 64, 1024], P('rows', 'cols'), may hold values from -0.1875 to 0.1875
- coarse_inverse: float32 [16384, 16384], P('rows', 'cols'), may hold values from -1 to 2.5, as said below
- stiff_diag: float32 [64, 4, 1024], P('rows', 'cols'), may hold values from 1 to 4
- nbr_index: int32 [64, 4, 80, 1024], P('rows', 'cols'), may hold values from 0 to 1023
- nbr_coef: float32 [64, 4, 80, 1024], P('rows', 'cols'), may hold values from -0.625 to 0.625
- send_rows: int32 [64, 4, 4, 128], P('rows', 'cols'), may hold values from 0 to 511
Outputs:
- solution: float32 [32, 131072], P(None, ('rows', 'cols'))
- residual: float32 [32, 131072], P(None, ('rows', 'cols'))
Inputs may be any that keep to these rules, and one draw needn't show every extreme that they name: `local_inverse`: each subdomain inverse has a diagonal between 0.25 and 2 and small off-diagonal entries. `coarse_inverse`: a diagonal between 0.25 and 2 at entries whose row and column name the same coarse unknown, small entries elsewhere.
All inputs are finite; a program needn't handle non-finite values.
Results may differ from a plain program's by a relative error of at most 0.00013.
Values sent between devices are 32-bit elements; how exact they have to be, the bound alone decides.
A program may use at most 128 MiB of HBM per device.

v0:
```python
import jax
import jax.numpy as jnp
from jax import lax
from jax.sharding import PartitionSpec as P


def from_behind(block, axis, distance):
    devices = range(lax.axis_size(axis))
    route = [(i - distance, i) for i in devices if i - distance in devices]
    return lax.ppermute(block, axis, route)


def along_rows(block, offset):
    return from_behind(block, "rows", offset)


def along_cols(block, offset):
    return from_behind(block, "cols", offset)


def extend(owned, sends):
    picked = [owned[:, sends[e]] for e in range(4)]
    first = along_rows(picked[0], 1)
    second = along_rows(picked[1], -1)
    third = along_cols(picked[2], 1)
    fourth = along_cols(picked[3], -1)
    return jnp.concatenate([owned, first, second, third, fourth], axis=1)


def fold(sub, sends, own_count, block_rows):
    owned = sub[:, :own_count]
    bands = [
        sub[:, own_count + e * block_rows : own_count + (e + 1) * block_rows] for e in range(4)
    ]
    backs = [
        along_rows(bands[0], -1),
        along_rows(bands[1], 1),
        along_cols(bands[2], -1),
        along_cols(bands[3], 1),
    ]
    for e in range(4):
        owned = owned.at[:, sends[e]].add(backs[e])
    return owned


def coarse_apply(restricted, coarse_block):
    highest = lax.Precision.HIGHEST
    partial_sum = lax.dot_general(
        lax.all_gather(restricted, "rows", axis=1, tiled=True),
        coarse_block,
        (((1,), (1,)), ((), ())),
        precision=highest,
        preferred_element_type=jnp.float32,
    )
    return lax.psum_scatter(partial_sum, "cols", scatter_dimension=1, tiled=True)


def couple(sub, diag, index, coef):
    coupled = diag[None, :] * sub
    count = index.shape[0]
    group = min(16, count)
    for begin in range(0, count, group):
        finish = min(begin + group, count)
        nearby = sub[:, index[begin:finish]]
        coupled = coupled + jnp.sum(nearby * coef[None, begin:finish, :], axis=1)
    return coupled


def body(
    right_side, local_inverse, modes, coarse_inverse, stiff_diag, nbr_index, nbr_coef, send_rows
):
    highest = lax.Precision.HIGHEST
    inverse = local_inverse[0, 0]
    basis = modes[0, 0]
    diag = stiff_diag[0, 0]
    index = nbr_index[0, 0]
    coef = nbr_coef[0, 0]
    sends = send_rows[0, 0]
    own_count = right_side.shape[1]
    block_rows = sends.shape[1]

    def precondition(resid):
        sub = extend(resid, sends)
        local = lax.dot_general(
            sub,
            inverse,
            (((1,), (1,)), ((), ())),
            precision=highest,
            preferred_element_type=jnp.float32,
        )
        restricted = lax.dot_general(
            sub,
            basis,
            (((1,), (1,)), ((), ())),
            precision=highest,
            preferred_element_type=jnp.float32,
        )
        coarse = coarse_apply(restricted, coarse_inverse)
        local = local + jnp.dot(
            coarse, basis, precision=highest, preferred_element_type=jnp.float32
        )
        return fold(local, sends, own_count, block_rows)

    first = precondition(right_side)
    sub = extend(first, sends)
    coupled = couple(sub, diag, index, coef)
    image = fold(coupled, sends, own_count, block_rows)
    residual = right_side - image
    solution = first + precondition(residual)
    return (solution, residual)


def solution(mesh):
    in_specs = (
        P(None, ("rows", "cols")),
        P("rows", "cols", None, None),
        P("rows", "cols", None, None),
        P("rows", "cols"),
        P("rows", "cols", None),
        P("rows", "cols", None, None),
        P("rows", "cols", None, None),
        P("rows", "cols", None, None),
    )
    out_specs = (P(None, ("rows", "cols")), P(None, ("rows", "cols")))
    return jax.shard_map(body, mesh=mesh, in_specs=in_specs, out_specs=out_specs, check_vma=False)
```

profile of v0, /device:TPU:1, one launch (start us, length us, event | category | flops | bytes accessed | tf_op | source)
XLA Modules:
  0.0 823.2 jit_solution(2240018692300086383)
XLA Ops:
  9.7 4.4 collective-permute-start
  16.7 5.7 collective-permute-start.2
  27.2 2.9 collective-permute-done.3
  30.5 137.0 %all-gather = f32[64,64,32]{1,2,0:T(8,128)S(1)} all-gather(f32[1,64,32]{1,2,0:T(8,128)S(1)} %convolution_bitcast_fusion.3), channel_id=1, replica_groups=mesh['rows'=64,'cols'=4] {'rows'}, dimensions={0}, use_global_device_ids=true | all-gather | bytes 532480 | tf_op jit(solution)/shard_map/all_gather | solution.py:49
  168.4 5.8 convolution_bitcast_fusion.1
  174.3 50.1 %reduce-scatter.7.cloned.1.call-done = f32[64,32]{1,0:T(8,128)} async-done(((f32[256,32]{1,0:T(8,128)}), f32[64,32]{1,0:T(8,128)}) %reduce-scatter.7.cloned.1.call-update) | async-done | bytes 8208
  225.5 6.0 fusion.4
  231.5 3.4 collective-permute-start.7
  236.9 2.9 collective-permute-start.5
  241.3 3.0 collective-permute-done.4
  250.8 3.2 collective-permute-start.8
  257.3 6.9 collective-permute-start.10
  266.4 4.9 collective-permute-done.11
  271.3 54.4 %gather_fusion.12 = f32[16384,32]{1,0:T(8,128)} fusion(f32[32,1024]{0,1:T(8,128)S(1)} %constant_dynamic-update-slice_fusion.5, s32[16384]{0:T(1024)S(1)} %broadcast_clamp_fusion), kind=kCustom, calls=%fused_computation.12 | custom fusion | bytes 4259840 | tf_op jit(solution)/shard_map/gather | solution.py:64
  325.7 54.4 %gather_fusion.11 = f32[16384,32]{1,0:T(8,128)} fusion(f32[32,1024]{0,1:T(8,128)S(1)} %constant_dynamic-update-slice_fusion.5, s32[16384]{0:T(1024)S(1)} %broadcast_clamp_fusion.1), kind=kCustom, calls=%fused_computation.11 | custom fusion | bytes 4259840 | tf_op jit(solution)/shard_map/gather | solution.py:64
  380.1 54.4 %gather_fusion.10 = f32[16384,32]{1,0:T(8,128)} fusion(f32[32,1024]{0,1:T(8,128)S(1)} %constant_dynamic-update-slice_fusion.5, s32[16384]{0:T(1024)S(1)} %broadcast_clamp_fusion.2), kind=kCustom, calls=%fused_computation.10 | custom fusion | bytes 4259840 | tf_op jit(solution)/shard_map/gather | solution.py:64
  434.5 54.4 %gather_fusion.9 = f32[16384,32]{1,0:T(8,128)} fusion(f32[32,1024]{0,1:T(8,128)S(1)} %constant_dynamic-update-slice_fusion.5, s32[16384]{0:T(1024)S(1)} %broadcast_clamp_fusion.3), kind=kCustom, calls=%fused_computation.9 | custom fusion | bytes 4259840 | tf_op jit(solution)/shard_map/gather | solution.py:64
  488.8 54.3 %gather_fusion.8 = f32[16384,32]{1,0:T(8,128)} fusion(f32[32,1024]{0,1:T(8,128)S(1)} %constant_dynamic-update-slice_fusion.5, s32[16384]{0:T(1024)S(1)} %broadcast_clamp_fusion.4), kind=kCustom, calls=%fused_computation.8 | custom fusion | bytes 4259840 | tf_op jit(solution)/shard_map/gather | solution.py:64
  543.2 5.6 multiply_reduce_fusion
  548.8 5.4 multiply_reduce_fusion.1
  563.4 5.2 collective-permute-start.13
  570.5 5.1 collective-permute-start.15
  584.0 4.8 collective-permute-start.16
  590.1 3.1 collective-permute-start.18
  595.5 4.9 collective-permute-done.19
  600.8 132.9 %all-gather.1 = f32[64,64,32]{1,2,0:T(8,128)S(1)} all-gather(f32[1,64,32]{1,2,0:T(8,128)S(1)} %convolution_bitcast_fusion.2), channel_id=1, replica_groups=mesh['rows'=64,'cols'=4] {'rows'}, dimensions={0}, use_global_device_ids=true | all-gather | bytes 532480 | tf_op jit(solution)/shard_map/all_gather | solution.py:49
  734.7 5.8 convolution_bitcast_fusion
  740.6 49.2 %reduce-scatter.9.cloned.1.call-done = f32[64,32]{1,0:T(8,128)} async-done(((f32[256,32]{1,0:T(8,128)}), f32[64,32]{1,0:T(8,128)}) %reduce-scatter.9.cloned.1.call-update) | async-done | bytes 8208
  790.8 6.0 fusion.7
  796.9 3.5 collective-permute-start.23
  802.3 2.9 collective-permute-start.21
  806.6 3.0 collective-permute-done.20
  (150 shorter events, 62.7 us)
Async XLA Ops:
  7.2 23.0 %copy-start = (f32[1,1,64,1024]{3,2,1,0:T(8,128)S(1)}, f32[1,1,64,1024]{3,2,1,0:T(8,128)}, u32[]{:S(2)}) copy-start(f32[1,1,64,1024]{3,2,1,0:T(8,128)} %param.10) | copy-start | bytes 786436
  7.2 217.2 %reduce-scatter.7.cloned.1.call-start = ((), (), s32[]{:S(2)}) async-start(), calls=%async_computation.2 | async-start | bytes 163840
  9.7 17.3 %collective-permute-start = (f32[32,128]{0,1:T(8,128)S(1)}, f32[32,128]{0,1:T(8,128)S(1)}, u32[]{:S(2)}, u32[]{:S(2)}) collective-permute-start(f32[32,128]{0,1:T(8,128)S(1)} %bitcast.186), channel_id=1, source_target_pairs={{0,4},{4,8},{8,12},{12,16},{16,20},{20,24},{24,28},{28,32},{32,36}... | collective-permute-start | bytes 49160 | tf_op jit(solution)/shard_map/ppermute | solution.py:10
  14.7 12.3 %collective-permute-start.1 = (f32[32,128]{0,1:T(8,128)S(1)}, f32[32,128]{0,1:T(8,128)S(1)}, u32[]{:S(2)}, u32[]{:S(2)}) collective-permute-start(f32[32,128]{0,1:T(8,128)S(1)} %bitcast.183), channel_id=1, source_target_pairs={{4,0},{8,4},{12,8},{16,12},{20,16},{24,20},{28,24},{32,28},{36,32}... | collective-permute-start | bytes 49160 | tf_op jit(solution)/shard_map/ppermute | solution.py:10
  16.7 10.5 %collective-permute-start.2 = (f32[32,128]{0,1:T(8,128)S(1)}, f32[32,128]{0,1:T(8,128)S(1)}, u32[]{:S(2)}, u32[]{:S(2)}) collective-permute-start(f32[32,128]{0,1:T(8,128)S(1)} %bitcast.184), channel_id=1, source_target_pairs={{0,1},{1,2},{2,3},{4,5},{5,6},{6,7},{8,9},{9,10},{10,11},{12,13},{... | collective-permute-start | bytes 49160 | tf_op jit(solution)/shard_map/ppermute | solution.py:10
  23.0 7.1 collective-permute-start.3
  26.0 215.1 %copy-start.2 = (f32[1,1,80,1024]{3,2,1,0:T(8,128)S(1)}, f32[1,1,80,1024]{3,2,1,0:T(8,128)}, u32[]{:S(2)}) copy-start(f32[1,1,80,1024]{3,2,1,0:T(8,128)} %param.14) | copy-start | bytes 983044
  174.3 615.5 %reduce-scatter.9.cloned.1.call-start = ((), (), s32[]{:S(2)}) async-start(), calls=%async_computation.3 | async-start | bytes 163840
  231.5 13.1 %collective-permute-start.7 = (f32[32,128]{1,0:T(8,128)S(1)}, f32[32,128]{1,0:T(8,128)S(1)}, u32[]{:S(2)}, u32[]{:S(2)}) collective-permute-start(f32[32,128]{1,0:T(8,128)S(1)} %get-tuple-element.28), channel_id=1, source_target_pairs={{0,1},{1,2},{2,3},{4,5},{5,6},{6,7},{8,9},{9,10},{10,11},{12,13},{... | collective-permute-start | bytes 49160 | tf_op jit(solution)/shard_map/ppermute | solution.py:10
  235.0 9.5 %collective-permute-start.6 = (f32[32,128]{1,0:T(8,128)S(1)}, f32[32,128]{1,0:T(8,128)S(1)}, u32[]{:S(2)}, u32[]{:S(2)}) collective-permute-start(f32[32,128]{1,0:T(8,128)S(1)} %get-tuple-element.29), channel_id=1, source_target_pairs={{1,0},{2,1},{3,2},{5,4},{6,5},{7,6},{9,8},{10,9},{11,10},{13,12},{... | collective-permute-start | bytes 49160 | tf_op jit(solution)/shard_map/ppermute | solution.py:10
  236.9 7.5 collective-permute-start.5
  239.8 4.5 collective-permute-start.4
  250.8 15.4 %collective-permute-start.8 = (f32[32,128]{0,1:T(8,128)S(1)}, f32[32,128]{0,1:T(8,128)S(1)}, u32[]{:S(2)}, u32[]{:S(2)}) collective-permute-start(f32[32,128]{0,1:T(8,128)S(1)} %bitcast.191), channel_id=1, source_target_pairs={{0,4},{4,8},{8,12},{12,16},{16,20},{20,24},{24,28},{28,32},{32,36}... | collective-permute-start | bytes 49160 | tf_op jit(solution)/shard_map/ppermute | solution.py:10
  256.0 10.3 %collective-permute-start.9 = (f32[32,128]{0,1:T(8,128)S(1)}, f32[32,128]{0,1:T(8,128)S(1)}, u32[]{:S(2)}, u32[]{:S(2)}) collective-permute-start(f32[32,128]{0,1:T(8,128)S(1)} %bitcast.193), channel_id=1, source_target_pairs={{4,0},{8,4},{12,8},{16,12},{20,16},{24,20},{28,24},{32,28},{36,32}... | collective-permute-start | bytes 49160 | tf_op jit(solution)/shard_map/ppermute | solution.py:10
  257.3 9.0 %collective-permute-start.10 = (f32[32,128]{0,1:T(8,128)S(1)}, f32[32,128]{0,1:T(8,128)S(1)}, u32[]{:S(2)}, u32[]{:S(2)}) collective-permute-start(f32[32,128]{0,1:T(8,128)S(1)} %bitcast.190), channel_id=1, source_target_pairs={{0,1},{1,2},{2,3},{4,5},{5,6},{6,7},{8,9},{9,10},{10,11},{12,13},{... | collective-permute-start | bytes 49160 | tf_op jit(solution)/shard_map/ppermute | solution.py:10
  264.2 7.1 collective-permute-start.11
  543.2 11.1 %copy-start.1 = (f32[16384,32]{1,0:T(8,128)S(1)}, f32[16384,32]{1,0:T(8,128)}, u32[]{:S(2)}) copy-start(f32[16384,32]{1,0:T(8,128)} %gather_fusion.10) | copy-start | bytes 6291460
  548.8 8.0 slice-start.2
  554.2 5.1 slice-start
  562.1 13.6 %collective-permute-start.12 = (f32[32,128]{0,1:T(8,128)S(1)}, f32[32,128]{0,1:T(8,128)S(1)}, u32[]{:S(2)}, u32[]{:S(2)}) collective-permute-start(f32[32,128]{0,1:T(8,128)S(1)} %get-tuple-element.13), channel_id=1, source_target_pairs={{4,0},{8,4},{12,8},{16,12},{20,16},{24,20},{28,24},{32,28},{36,32}... | collective-permute-start | bytes 49160 | tf_op jit(solution)/shard_map/ppermute | solution.py:10
  563.4 13.7 %collective-permute-start.13 = (f32[32,128]{0,1:T(8,128)S(1)}, f32[32,128]{0,1:T(8,128)S(1)}, u32[]{:S(2)}, u32[]{:S(2)}) collective-permute-start(f32[32,128]{0,1:T(8,128)S(1)} %get-tuple-element.12), channel_id=1, source_target_pairs={{0,4},{4,8},{8,12},{12,16},{16,20},{20,24},{24,28},{28,32},{32,36}... | collective-permute-start | bytes 49160 | tf_op jit(solution)/shard_map/ppermute | solution.py:10
  568.6 9.9 %collective-permute-start.14 = (f32[32,128]{0,1:T(8,128)S(1)}, f32[32,128]{0,1:T(8,128)S(1)}, u32[]{:S(2)}, u32[]{:S(2)}) collective-permute-start(f32[32,128]{0,1:T(8,128)S(1)} %get-tuple-element.11), channel_id=1, source_target_pairs={{1,0},{2,1},{3,2},{5,4},{6,5},{7,6},{9,8},{10,9},{11,10},{13,12},{... | collective-permute-start | bytes 49160 | tf_op jit(solution)/shard_map/ppermute | solution.py:10
  570.5 9.4 %collective-permute-start.15 = (f32[32,128]{0,1:T(8,128)S(1)}, f32[32,128]{0,1:T(8,128)S(1)}, u32[]{:S(2)}, u32[]{:S(2)}) collective-permute-start(f32[32,128]{0,1:T(8,128)S(1)} %get-tuple-element.10), channel_id=1, source_target_pairs={{0,1},{1,2},{2,3},{4,5},{5,6},{6,7},{8,9},{9,10},{10,11},{12,13},{... | collective-permute-start | bytes 49160 | tf_op jit(solution)/shard_map/ppermute | solution.py:10
  584.0 225.8 %copy-start.3 = (f32[32,512]{1,0:T(8,128)}, f32[32,512]{1,0:T(8,128)S(1)}, u32[]{:S(2)}) copy-start(f32[32,512]{1,0:T(8,128)S(1)} %copy.111) | copy-start | bytes 196612
  584.0 11.3 %collective-permute-start.16 = (f32[32,128]{0,1:T(8,128)S(1)}, f32[32,128]{0,1:T(8,128)S(1)}, u32[]{:S(2)}, u32[]{:S(2)}) collective-permute-start(f32[32,128]{0,1:T(8,128)S(1)} %bitcast.192), channel_id=1, source_target_pairs={{0,4},{4,8},{8,12},{12,16},{16,20},{20,24},{24,28},{28,32},{32,36}... | collective-permute-start | bytes 49160 | tf_op jit(solution)/shard_map/ppermute | solution.py:10
  588.8 6.5 collective-permute-start.17
  590.1 5.3 collective-permute-start.18
  593.3 7.1 collective-permute-start.19
  796.9 13.1 %collective-permute-start.23 = (f32[32,128]{1,0:T(8,128)S(1)}, f32[32,128]{1,0:T(8,128)S(1)}, u32[]{:S(2)}, u32[]{:S(2)}) collective-permute-start(f32[32,128]{1,0:T(8,128)S(1)} %get-tuple-element.24), channel_id=1, source_target_pairs={{0,1},{1,2},{2,3},{4,5},{5,6},{6,7},{8,9},{9,10},{10,11},{12,13},{... | collective-permute-start | bytes 49160 | tf_op jit(solution)/shard_map/ppermute | solution.py:10
  800.3 9.5 %collective-permute-start.22 = (f32[32,128]{1,0:T(8,128)S(1)}, f32[32,128]{1,0:T(8,128)S(1)}, u32[]{:S(2)}, u32[]{:S(2)}) collective-permute-start(f32[32,128]{1,0:T(8,128)S(1)} %get-tuple-element.25), channel_id=1, source_target_pairs={{1,0},{2,1},{3,2},{5,4},{6,5},{7,6},{9,8},{10,9},{11,10},{13,12},{... | collective-permute-start | bytes 49160 | tf_op jit(solution)/shard_map/ppermute | solution.py:10
  802.3 7.5 collective-permute-start.21
  805.2 4.5 collective-permute-start.20
  (3 other events, 10.1 us)
Sparse Core Ops, SparseCore 0:
  174.4 49.9 reduce-scatter.6
  740.6 49.1 reduce-scatter.8
where the time goes:
time: 827 us; the launch traced here: 823 us
  local copies, waits for them, and re-layouts  286 us (35%)
  blocking collectives  270 us (33%)
  waiting for transfers between devices  118 us (14%)
  starting transfers between devices  70.6 us (9%)
  other arithmetic  37.1 us (4%)
  matrix products  26.5 us (3%)
  between operations  15 us (2%)
    gather x5, local copies, waits for them, and re-layouts, couple(): nearby = sub[:, index[begin:finish]]  272 us
    all_gather x2, blocking collectives, coarse_apply(): lax.all_gather(restricted, 'rows', axis=1, tiled=True)  270 us
    unnamed x4, waiting for transfers between devices  99.3 us
    ppermute x24, starting transfers between devices, from_behind(): return lax.ppermute(block, axis, route)  70.6 us
    ppermute x24, waiting for transfers between devices, from_behind(): return lax.ppermute(block, axis, route)  18.8 us
    reduce_sum x5, other arithmetic, couple(): coupled = coupled + jnp.sum(nearby * coef[None, begin:finish, :], axis=1)  18.5 us
  transfers between devices with their start and end apart: 26, of which 7 were waited for; matrix products, arithmetic and copies ran while one was open for 1% of the time, Pallas kernels for 0%

commit v1 on v0

v1 whole, which is shorter than its diff:
```python
import jax
import jax.numpy as jnp
from jax import lax
from jax.experimental import pallas as pl
from jax.experimental.pallas import tpu as pltpu
from jax.sharding import PartitionSpec as P

BF = jnp.bfloat16
F32 = jnp.float32
NT = (((1,), (1,)), ((), ()))
NN = (((1,), (0,)), ((), ()))
UNROLL = 64


def dot(a, b, dims):
    return lax.dot_general(a, b, dims, preferred_element_type=F32)


def halves(x):
    hi = x.astype(BF)
    return hi, (x - hi.astype(F32)).astype(BF)


def split_into(src, high, low, rows, step):
    def part(t, carry):
        at = pl.ds(pl.multiple_of(t * step, step), step)
        hi, lo = halves(src[at, :])
        high[at, :] = hi
        low[at, :] = lo
        return carry

    lax.fori_loop(0, rows // step, part, 0)


def dot_twice(x, w, dims):
    n = x.shape[0]
    hi, lo = halves(x)
    both = dot(jnp.concatenate([hi, lo], 0), w, dims)
    return both[:n] + both[n:]


def dot_thrice(x, high, low, dims):
    n = x.shape[0]
    hi, lo = halves(x)
    both = dot(jnp.concatenate([hi, lo], 0), high, dims)
    return both[:n] + both[n:] + dot(hi, low, dims)


def kernel(
    rhs_ref, inv_hbm, modes_hbm, coarse_hbm, diag_ref, index_hbm, coef_hbm, sends_ref,
    sol_ref, res_ref,
    inv_raw, coarse_raw, modes_raw, index_raw, coef_raw,
    inv_hi, inv_lo, coarse_hi, coarse_lo, modes_hi, modes_lo,
    pick_mat, low_t, high_t, coef_hi, coef_lo, tiles, stiff_hi, stiff_lo,
    x_hi, halo_out, halo_in, gathered, parts, others, local_buf, first_buf,
    load_sem, halo_send, halo_recv, y_send, y_recv, z_send, z_recv, x_send, x_recv,
    col_send, col_recv,
):
    i = lax.axis_index("rows")
    j = lax.axis_index("cols")
    gx = i // 16
    gy = lax.rem(i // 8, 2)
    gz = lax.rem(i, 8)

    def row_of(x, y, z):
        return x * 16 + y * 8 + z

    loads = [
        pltpu.make_async_copy(s, d, load_sem.at[n])
        for n, (s, d) in enumerate(
            [
                (modes_hbm, modes_raw),
                (index_hbm, index_raw),
                (coef_hbm, coef_raw),
                (inv_hbm, inv_raw),
                (coarse_hbm, coarse_raw),
            ]
        )
    ]
    for load in loads:
        load.start()

    beside = [
        (lax.rem(i + 1, 64), j),
        (lax.rem(i + 63, 64), j),
        (i, lax.rem(j + 1, 4)),
        (i, lax.rem(j + 3, 4)),
    ]
    y_peer = (row_of(gx, 1 - gy, gz), j)

    def z_peer(d):
        return (row_of(gx, gy, lax.rem(gz + d, 8)), j)

    def x_peer(d):
        return (row_of(lax.rem(gx + d, 4), gy, gz), j)

    barrier = pltpu.get_barrier_semaphore()
    greet = beside + [(i, lax.rem(j + 2, 4)), y_peer]
    greet = greet + [z_peer(d) for d in range(1, 8)] + [x_peer(d) for d in range(1, 4)]
    for peer in greet:
        pl.semaphore_signal(barrier, inc=1, device_id=peer, device_id_type=pl.DeviceIdType.MESH)

    row_ids = lax.broadcasted_iota(jnp.int32, (512, 128), 0)
    for e in range(4):
        hit = row_ids == jnp.broadcast_to(sends_ref[e : e + 1, :], (512, 128))
        pick_mat[:, e * 128 : (e + 1) * 128] = jnp.where(hit, 1.0, 0.0).astype(BF)

    has = [i > 0, i < 63, j > 0, j < 3]

    def halo_copy(k, e, way):
        return pltpu.make_async_remote_copy(
            src_ref=halo_out.at[k, e],
            dst_ref=halo_in.at[k, e],
            send_sem=halo_send.at[k, e],
            recv_sem=halo_recv.at[k, e],
            device_id=beside[way],
            device_id_type=pl.DeviceIdType.MESH,
        )

    def halo_start(k, values, back):
        for e in range(4):
            halo_out[k, e] = values[:, e * 128 : (e + 1) * 128]
            halo_copy(k, e, e ^ back).start()

    def halo_wait(k, back):
        got = []
        for e in range(4):
            halo_copy(k, e, e ^ back).wait_recv()
            got.append(jnp.where(has[e ^ back], halo_in[k, e], 0.0))
        return jnp.concatenate(got, 1)

    lane = lax.broadcasted_iota(jnp.int32, (16, 128), 1)
    left = lane < 64

    def pair_at(x, z):
        return pl.ds(x * 16 + z * 2, 2)

    def remote(src, dst, send, recv, peer):
        return pltpu.make_async_remote_copy(
            src_ref=src,
            dst_ref=dst,
            send_sem=send,
            recv_sem=recv,
            device_id=peer,
            device_id_type=pl.DeviceIdType.MESH,
        )

    def y_copy(k, y):
        at = gathered.at[k, pl.ds(gx * 16 + gz * 2 + y, 1)]
        return remote(at, at, y_send.at[k], y_recv.at[k], y_peer)

    def z_copy(k, d, z):
        at = gathered.at[k, pair_at(gx, z)]
        return remote(at, at, z_send.at[k, d], z_recv.at[k, d], z_peer(d))

    def x_copy(k, d, dx, x):
        at = gathered.at[k, pair_at(x, lax.rem(gz - d + 8, 8))]
        return remote(at, at, x_send.at[k, d, dx], x_recv.at[k, d, dx], x_peer(dx))

    def col_copy(k, d, slot):
        return remote(
            parts.at[k, slot],
            others.at[k, d],
            col_send.at[k, d],
            col_recv.at[k, d],
            (i, lax.rem(j + d, 4)),
        )

    def gather_start(k, restricted):
        block = jnp.where(left, restricted[:16], restricted[16:])
        gathered[k, pl.ds(gx * 16 + gz * 2 + gy, 1)] = block.reshape(1, 16, 128)
        y_copy(k, gy).start()

    def gather_spread(k, work):
        y_copy(k, 1 - gy).wait_recv()
        for d in (1, 7, 2, 6, 3, 5, 4):
            z_copy(k, d, gz).start()
        for dx in (1, 3, 2):
            x_copy(k, 0, dx, gx).start()
        work(0)

        def step(t, carry):
            d = jnp.where(lax.rem(t, 2) == 1, (t + 1) // 2, 8 - t // 2)
            z_copy(k, d, lax.rem(gz - d + 8, 8)).wait_recv()
            for dx in (1, 3, 2):
                x_copy(k, d, dx, gx).start()
            work(t)
            return carry

        lax.fori_loop(1, 8, step, 0)

    def gather_finish(k):
        def step(d, carry):
            for dx in (1, 3, 2):
                x_copy(k, d, dx, lax.rem(gx - dx + 4, 4)).wait_recv()
            return carry

        lax.fori_loop(0, 8, step, 0)

    def coarse_apply(k):
        for x in range(4):
            for y in range(2):
                for zz in range(4):
                    a = gathered[k, x * 16 + zz * 4 + y]
                    b = gathered[k, x * 16 + zz * 4 + 2 + y]
                    top = jnp.where(left, a, pltpu.roll(b, 64, 1))
                    low = jnp.where(left, pltpu.roll(a, 64, 1), b)
                    hi, lo = halves(jnp.concatenate([top, low], 0))
                    at = pl.ds((x * 8 + y * 4 + zz) * 128, 128)
                    x_hi[0:32, at] = hi
                    x_hi[32:64, at] = lo
        both = dot(x_hi[...], coarse_hi[...], NT)
        part = both[:32] + both[32:] + dot(x_hi[0:32, :], coarse_lo[...], NT)
        for c in range(4):
            a = part[:16, (c // 2) * 128 : (c // 2) * 128 + 128]
            b = part[16:, (c // 2) * 128 : (c // 2) * 128 + 128]
            if c % 2 == 0:
                packed = jnp.where(left, a, pltpu.roll(b, 64, 1))
            else:
                packed = jnp.where(left, pltpu.roll(a, 64, 1), b)
            parts[k, c] = packed
        for d in (2, 1, 3):
            col_copy(k, d, lax.rem(j + d, 4)).start()

    def coarse_finish(k):
        total = parts[k, j]
        for d in (1, 3, 2):
            col_copy(k, d, lax.rem(j + d, 4)).wait_recv()
            total = total + others[k, d]
        zero = jnp.zeros_like(total)
        return jnp.concatenate([jnp.where(left, total, zero), jnp.where(left, zero, total)], 0)

    def restrict(own, cols):
        return dot_thrice(own, modes_hi[:, cols], modes_lo[:, cols], NT)

    own_cols = slice(0, 512)
    rim_cols = slice(512, 1024)

    def pick(field):
        return dot_twice(field, pick_mat[...], NN)

    def scatter(bands):
        return dot_twice(bands, pick_mat[...], NT)

    rhs = rhs_ref[...]
    picked = pick(rhs)
    pl.semaphore_wait(barrier, len(greet))
    halo_start(0, picked, 0)

    loads[0].wait()
    m_hi, m_lo = halves(modes_raw[...])
    modes_hi[...] = jnp.concatenate([m_hi, m_hi], 0)
    modes_lo[...] = jnp.concatenate([m_lo, m_lo], 0)

    def stiff_prepare():
        loads[1].wait()
        loads[2].wait()

        def turn(t, carry):
            at = pl.ds(pl.multiple_of(t * 128, 128), 128)
            idx = jnp.concatenate([index_raw[:, at], jnp.zeros((48, 128), jnp.int32)], 0).T
            val = jnp.concatenate([coef_raw[:, at], jnp.zeros((48, 128), F32)], 0).T
            low_t[at, :] = (idx & 127).astype(F32)
            high_t[at, :] = (idx >> 7).astype(F32)
            hi = val.astype(BF).astype(F32)
            coef_hi[at, :] = hi
            coef_lo[at, :] = val - hi
            return carry

        lax.fori_loop(0, 8, turn, 0)

    def stiff_build(t):
        lanes = lax.broadcasted_iota(jnp.int32, (128, 128), 0).astype(F32).astype(BF)
        blocks = lax.broadcasted_iota(jnp.int32, (8, 128), 0).astype(F32)
        one = jnp.ones((128, 128), BF)
        none = jnp.zeros((128, 128), BF)
        blank = jnp.zeros((16, 128), BF)

        def some(g, carry):
            for q in range(UNROLL // 4):
                hot = []
                val = []
                s = t * 128 + g * UNROLL + q * 4
                for r in range(4):
                    at = pl.ds(s + r, 1)
                    low = jnp.broadcast_to(low_t[at, :], (128, 128)).astype(BF)
                    hot.append(jnp.where(low == lanes, one, none))
                    hit = jnp.broadcast_to(high_t[at, :], (8, 128)) == blocks
                    pair = [jnp.where(hit, coef_hi[at, :], 0.0), jnp.where(hit, coef_lo[at, :], 0.0)]
                    val.append(jnp.concatenate(pair, 0).astype(BF))
                right = jnp.concatenate(
                    [jnp.concatenate(hot[:2], 1), jnp.concatenate(hot[2:], 1)], 0
                )
                rows = [
                    jnp.concatenate([val[r], blank] if r % 2 == 0 else [blank, val[r]], 1)
                    for r in range(4)
                ]
                out = dot(jnp.concatenate(rows, 0), right, NT)
                for r in range(4):
                    cut = out[16 * r : 16 * r + 16, (r // 2) * 128 : (r // 2) * 128 + 128]
                    tiles[pl.ds(pl.multiple_of((s + r) * 8, 8), 8), :] = cut[:8] + cut[8:]
            return carry

        lax.fori_loop(0, 128 // UNROLL, some, 0)

    def stiff_finish():
        for r in range(4):
            for c in range(8):
                hi, lo = halves(tiles[pl.ds(c + r * 2048, 256, stride=8), :])
                stiff_hi[r * 256 : r * 256 + 256, c * 128 : c * 128 + 128] = hi
                stiff_lo[r * 256 : r * 256 + 256, c * 128 : c * 128 + 128] = lo

    def precondition(k, resid, ext_k, fold_k, prepare, work, late):
        restricted = restrict(resid, own_cols)
        prepare()
        rim = halo_wait(ext_k, 0)
        gather_start(k, restricted + restrict(rim, rim_cols))
        gather_spread(k, work)
        late()
        local_buf[...] = dot_thrice(
            jnp.concatenate([resid, rim], 1), inv_hi[...], inv_lo[...], NT
        )
        gather_finish(k)
        coarse_apply(k)
        if k == 0:
            stiff_finish()
        spread = coarse_finish(k)
        bands = local_buf[:, rim_cols] + dot_thrice(
            spread, modes_hi[:, rim_cols], modes_lo[:, rim_cols], NN
        )
        halo_start(fold_k, bands, 1)
        own = local_buf[:, own_cols] + dot_thrice(
            spread, modes_hi[:, own_cols], modes_lo[:, own_cols], NN
        )
        return own + scatter(halo_wait(fold_k, 1))

    def late_first():
        loads[3].wait()
        split_into(inv_raw, inv_hi, inv_lo, 1024, 128)
        loads[4].wait()
        split_into(coarse_raw, coarse_hi, coarse_lo, 256, 32)

    first = precondition(0, rhs, 0, 1, stiff_prepare, stiff_build, late_first)
    halo_start(2, pick(first), 0)
    first_buf[...] = first
    part = dot_thrice(first, stiff_hi[:, own_cols], stiff_lo[:, own_cols], NT)
    rim = halo_wait(2, 0)
    diag = diag_ref[...]
    bands = part[:, rim_cols] + diag[:, rim_cols] * rim + dot_thrice(
        rim, stiff_hi[rim_cols, rim_cols], stiff_lo[rim_cols, rim_cols], NT
    )
    halo_start(3, bands, 1)
    own = part[:, own_cols] + diag[:, own_cols] * first + dot_thrice(
        rim, stiff_hi[own_cols, rim_cols], stiff_lo[own_cols, rim_cols], NT
    )
    residual = rhs - (own + scatter(halo_wait(3, 1)))
    halo_start(4, pick(residual), 0)
    res_ref[...] = residual

    def nothing(*unused):
        return None

    second = precondition(1, residual, 4, 5, nothing, nothing, nothing)
    sol_ref[...] = first_buf[...] + second

    for k in range(6):
        for e in range(4):
            halo_copy(k, e, e ^ (k % 2)).wait_send()
    for k in range(2):
        y_copy(k, gy).wait_send()
        for d in range(1, 4):
            col_copy(k, d, lax.rem(j + d, 4)).wait_send()

        def drain_z(d, carry, k=k):
            z_copy(k, d, gz).wait_send()
            return carry

        def drain_x(d, carry, k=k):
            for dx in range(1, 4):
                x_copy(k, d, dx, gx).wait_send()
            return carry

        lax.fori_loop(1, 8, drain_z, 0)
        lax.fori_loop(0, 8, drain_x, 0)


def body(
    right_side, local_inverse, modes, coarse_inverse, stiff_diag, nbr_index, nbr_coef, send_rows
):
    vmem = pl.BlockSpec(memory_space=pltpu.VMEM)
    hbm = pl.BlockSpec(memory_space=pl.ANY)
    field = jax.ShapeDtypeStruct((32, 512), F32)
    dma = pltpu.SemaphoreType.DMA
    scratch = [
        pltpu.VMEM((1024, 1024), F32),
        pltpu.VMEM((256, 4096), F32),
        pltpu.VMEM((64, 1024), F32),
        pltpu.VMEM((80, 1024), jnp.int32),
        pltpu.VMEM((80, 1024), F32),
        pltpu.VMEM((1024, 1024), BF),
        pltpu.VMEM((1024, 1024), BF),
        pltpu.VMEM((256, 4096), BF),
        pltpu.VMEM((256, 4096), BF),
        pltpu.VMEM((128, 1024), BF),
        pltpu.VMEM((128, 1024), BF),
        pltpu.VMEM((512, 512), BF),
        pltpu.VMEM((1024, 128), F32),
        pltpu.VMEM((1024, 128), F32),
        pltpu.VMEM((1024, 128), F32),
        pltpu.VMEM((1024, 128), F32),
        pltpu.VMEM((8192, 128), F32),
        pltpu.VMEM((1024, 1024), BF),
        pltpu.VMEM((1024, 1024), BF),
        pltpu.VMEM((64, 4096), BF),
        pltpu.VMEM((6, 4, 32, 128), F32),
        pltpu.VMEM((6, 4, 32, 128), F32),
        pltpu.VMEM((2, 64, 16, 128), F32),
        pltpu.VMEM((2, 4, 16, 128), F32),
        pltpu.VMEM((2, 4, 16, 128), F32),
        pltpu.VMEM((32, 1024), F32),
        pltpu.VMEM((32, 512), F32),
        dma((5,)),
        dma((6, 4)),
        dma((6, 4)),
        dma((2,)),
        dma((2,)),
        dma((2, 8)),
        dma((2, 8)),
        dma((2, 8, 4)),
        dma((2, 8, 4)),
        dma((2, 4)),
        dma((2, 4)),
    ]
    return tuple(
        pl.pallas_call(
            kernel,
            out_shape=(field, field),
            in_specs=[vmem, hbm, hbm, hbm, vmem, hbm, hbm, vmem],
            out_specs=(vmem, vmem),
            scratch_shapes=scratch,
            compiler_params=pltpu.CompilerParams(
                collective_id=0, has_side_effects=True, vmem_limit_bytes=48 * 2**20
            ),
            name="schwarz",
        )(
            right_side,
            local_inverse[0, 0],
            modes[0, 0],
            coarse_inverse,
            stiff_diag[0],
            nbr_index[0, 0],
            nbr_coef[0, 0],
            send_rows[0, 0],
        )
    )


def solution(mesh):
    in_specs = (
        P(None, ("rows", "cols")),
        P("rows", "cols", None, None),
        P("rows", "cols", None, None),
        P("rows", "cols"),
        P("rows", "cols", None),
        P("rows", "cols", None, None),
        P("rows", "cols", None, None),
        P("rows", "cols", None, None),
    )
    out_specs = (P(None, ("rows", "cols")), P(None, ("rows", "cols")))
    return jax.shard_map(body, mesh=mesh, in_specs=in_specs, out_specs=out_specs, check_vma=False)
```

time: 827 us -> 94.6 us (0.11)
  local copies, waits for them, and re-layouts: 286 us -> 8.54 us
  blocking collectives: 270 us -> 0 us
  waiting for transfers between devices: 118 us -> 0 us
  Pallas kernels: 0 us -> 84.9 us
  starting transfers between devices: 70.6 us -> 0 us
  other arithmetic: 37.1 us -> 0 us
  matrix products: 26.5 us -> 0 us
  between operations: 15 us -> 0.66 us
    gather x17 -> x0, local copies, waits for them, and re-layouts: 280 us -> none  [the longest x5 272 us: couple(): nearby = sub[:, index[begin:finish]]]
    all_gather x2 -> x0, blocking collectives: 270 us -> none  [coarse_apply(): lax.all_gather(restricted, 'rows', axis=1, tiled=True)]
    unnamed x4 -> x0, waiting for transfers between devices: 99.3 us -> none
    pallas_call x0 -> x1, Pallas kernels: none -> 84.9 us  [body(): pl.pallas_call(kernel, out_shape=(field, field), in_specs=[vmem, hbm, hbm...]
    ppermute x24 -> x0, starting transfers between devices: 70.6 us -> none  [from_behind(): return lax.ppermute(block, axis, route)]
    ppermute x24 -> x0, waiting for transfers between devices: 18.8 us -> none  [from_behind(): return lax.ppermute(block, axis, route)]
    reduce_sum x5 -> x0, other arithmetic: 18.5 us -> none  [couple(): coupled = coupled + jnp.sum(nearby * coef[None, begin:finish, :], axis=1)]
    scatter-add x12 -> x0, other arithmetic: 16.4 us -> none  [fold(): owned = owned.at[:, sends[e]].add(backs[e])]
  transfers between devices with their start and end apart: 26 -> 0, of which waited for: 7 -> 0; matrix products, arithmetic and copies ran while one was open for 1% -> 0% of each run, Pallas kernels for 0% -> 0%
where the time goes in v1:
time: 94.6 us; the launch traced here: 94.1 us
  Pallas kernels  84.9 us (90%)
  local copies, waits for them, and re-layouts  8.54 us (9%)
    pallas_call x1, Pallas kernels, body(): pl.pallas_call(kernel, out_shape=(field, field), in_specs=[vmem, hbm, hbm...  84.9 us
    unnamed x16, local copies, waits for them, and re-layouts  8.54 us

profile of v1, /device:TPU:1, one launch (start us, length us, event | category | flops | bytes accessed | tf_op | source)
XLA Modules:
  0.0 94.1 jit_solution(14516359026577205625)
XLA Ops:
  0.6 0.0 copy-start
  0.6 2.2 %copy-done = f32[1,1,1024,1024]{3,2,1,0:T(8,128)S(1)} copy-done((f32[1,1,1024,1024]{3,2,1,0:T(8,128)S(1)}, f32[1,1,1024,1024]{3,2,1,0:T(8,128)}, u32[]{:S(2)}) %copy-start) | copy-done | bytes 4194328
  2.8 0.0 copy-start.1
  2.8 1.0 %copy-done.1 = s32[1,1,80,1024]{3,2,1,0:T(8,128)S(1)} copy-done((s32[1,1,80,1024]{3,2,1,0:T(8,128)S(1)}, s32[1,1,80,1024]{3,2,1,0:T(8,128)}, u32[]{:S(2)}) %copy-start.1) | copy-done | bytes 327704
  3.8 0.0 copy-start.2
  3.8 1.0 %copy-done.2 = f32[1,1,80,1024]{3,2,1,0:T(8,128)S(1)} copy-done((f32[1,1,80,1024]{3,2,1,0:T(8,128)S(1)}, f32[1,1,80,1024]{3,2,1,0:T(8,128)}, u32[]{:S(2)}) %copy-start.2) | copy-done | bytes 327704
  4.8 0.0 copy-start.3
  4.8 0.9 %copy-done.3 = f32[1,1,64,1024]{3,2,1,0:T(8,128)S(1)} copy-done((f32[1,1,64,1024]{3,2,1,0:T(8,128)S(1)}, f32[1,1,64,1024]{3,2,1,0:T(8,128)}, u32[]{:S(2)}) %copy-start.3) | copy-done | bytes 262168
  5.7 0.0 copy-start.4
  5.7 0.8 copy-done.4
  6.6 0.0 copy-start.5
  6.6 0.7 copy-done.5
  7.2 0.0 copy-start.6
  7.2 0.7 copy-done.6
  7.9 84.9 %schwarz.1 = (f32[32,512]{1,0:T(8,128)S(1)}, f32[32,512]{1,0:T(8,128)S(1)}) custom-call(f32[32,512]{1,0:T(8,128)S(1)} %copy-done.4, f32[1024,1024]{1,0:T(8,128)S(1)} %bitcast.6, f32[64,1024]{1,0:T(8,128)S(1)} %bitcast.9, f32[256,4096]{1,0:T(8,128)} %coarse_hbm.1, f32[1,1024]{1,0:T(1,128)S(1)} %bitcast.10, s32[80,1024]{1,0:T(8,128)S(1)} %bitcast.7, ...), custom_call_target="tpu_custom_call" | custom-call | tf_op jit(solution)/shard_map/schwarz/pallas_call | solution.py:435
  92.9 0.6 copy.12
  93.5 0.6 copy.13
Async XLA Ops:
  0.6 2.2 %copy-start = (f32[1,1,1024,1024]{3,2,1,0:T(8,128)S(1)}, f32[1,1,1024,1024]{3,2,1,0:T(8,128)}, u32[]{:S(2)}) copy-start(f32[1,1,1024,1024]{3,2,1,0:T(8,128)} %param.9) | copy-start | bytes 12582916
  2.8 1.0 %copy-start.1 = (s32[1,1,80,1024]{3,2,1,0:T(8,128)S(1)}, s32[1,1,80,1024]{3,2,1,0:T(8,128)}, u32[]{:S(2)}) copy-start(s32[1,1,80,1024]{3,2,1,0:T(8,128)} %param.13) | copy-start | bytes 983044
  3.8 1.0 %copy-start.2 = (f32[1,1,80,1024]{3,2,1,0:T(8,128)S(1)}, f32[1,1,80,1024]{3,2,1,0:T(8,128)}, u32[]{:S(2)}) copy-start(f32[1,1,80,1024]{3,2,1,0:T(8,128)} %param.14) | copy-start | bytes 983044
  4.8 0.9 %copy-start.3 = (f32[1,1,64,1024]{3,2,1,0:T(8,128)S(1)}, f32[1,1,64,1024]{3,2,1,0:T(8,128)}, u32[]{:S(2)}) copy-start(f32[1,1,64,1024]{3,2,1,0:T(8,128)} %param.10) | copy-start | bytes 786436
  5.7 0.8 copy-start.4
  6.6 0.7 copy-start.5
  7.2 0.7 copy-start.6

commit v2 on v1

v2 whole, which is shorter than its diff:
```python
import jax
import jax.numpy as jnp
from jax import lax
from jax.experimental import pallas as pl
from jax.experimental.pallas import tpu as pltpu
from jax.sharding import PartitionSpec as P

BF = jnp.bfloat16
F32 = jnp.float32
NT = (((1,), (1,)), ((), ()))
NN = (((1,), (0,)), ((), ()))
UNROLL = 64


def dot(a, b, dims):
    return lax.dot_general(a, b, dims, preferred_element_type=F32)


def halves(x):
    hi = x.astype(BF)
    return hi, (x - hi.astype(F32)).astype(BF)


def split_into(src, high, low, rows, step):
    def part(t, carry):
        at = pl.ds(pl.multiple_of(t * step, step), step)
        hi, lo = halves(src[at, :])
        high[at, :] = hi
        low[at, :] = lo
        return carry

    lax.fori_loop(0, rows // step, part, 0)


def dot_twice(x, w, dims):
    n = x.shape[0]
    hi, lo = halves(x)
    both = dot(jnp.concatenate([hi, lo], 0), w, dims)
    return both[:n] + both[n:]


def dot_thrice(x, high, low, dims):
    n = x.shape[0]
    hi, lo = halves(x)
    both = dot(jnp.concatenate([hi, lo], 0), high, dims)
    return both[:n] + both[n:] + dot(hi, low, dims)


def kernel(
    rhs_hbm, inv_hbm, modes_hbm, coarse_hbm, diag_hbm, index_hbm, coef_hbm, sends_hbm,
    sol_hbm, res_hbm,
    rhs_ref, diag_ref, sends_ref, inv_raw, coarse_raw, modes_raw, index_raw, coef_raw,
    inv_hi, inv_lo, coarse_hi, coarse_lo, modes_hi, modes_lo,
    pick_mat, pick_t, gram, res_buf, low_t, high_t, coef_hi, coef_lo, tiles, stiff_hi, stiff_lo,
    x_hi, halo_out, halo_in, gathered, parts, others, local_buf, first_buf,
    load_sem, halo_send, halo_recv, plane_send, plane_recv, x_send, x_recv,
    col_send, col_recv,
):
    i = lax.axis_index("rows")
    j = lax.axis_index("cols")
    gx = i // 16
    gy = lax.rem(i // 8, 2)
    gz = lax.rem(i, 8)

    def row_of(x, y, z):
        return x * 16 + y * 8 + z

    loads = [
        pltpu.make_async_copy(s, d, load_sem.at[n])
        for n, (s, d) in enumerate(
            [
                (sends_hbm, sends_ref),
                (rhs_hbm, rhs_ref),
                (modes_hbm, modes_raw),
                (diag_hbm, diag_ref),
                (index_hbm, index_raw),
                (coef_hbm, coef_raw),
                (inv_hbm, inv_raw),
                (coarse_hbm, coarse_raw),
            ]
        )
    ]
    for load in loads:
        load.start()

    beside = [
        (lax.rem(i + 1, 64), j),
        (lax.rem(i + 63, 64), j),
        (i, lax.rem(j + 1, 4)),
        (i, lax.rem(j + 3, 4)),
    ]

    def plane_peer(flip, d):
        return (row_of(gx, 1 - gy if flip else gy, lax.rem(gz + d, 8)), j)

    def x_peer(d):
        return (row_of(lax.rem(gx + d, 4), gy, gz), j)

    unsent = []
    barrier = pltpu.get_barrier_semaphore()
    greet = [plane_peer(flip, d) for d in (4, 3, 5, 2, 6, 1, 7, 0) for flip in (1, 0) if flip or d]
    greet = greet + [x_peer(d) for d in (2, 1, 3)] + beside + [(i, lax.rem(j + 2, 4))]
    for peer in greet:
        pl.semaphore_signal(barrier, inc=1, device_id=peer, device_id_type=pl.DeviceIdType.MESH)

    loads[0].wait()
    row_ids = lax.broadcasted_iota(jnp.int32, (512, 128), 0)
    for e in range(4):
        hit = row_ids == jnp.broadcast_to(sends_ref[e : e + 1, :], (512, 128))
        pick_mat[:, e * 128 : (e + 1) * 128] = jnp.where(hit, 1.0, 0.0).astype(BF)

    has = [i > 0, i < 63, j > 0, j < 3]

    def halo_copy(k, e, way):
        return pltpu.make_async_remote_copy(
            src_ref=halo_out.at[k, e],
            dst_ref=halo_in.at[k, e],
            send_sem=halo_send.at[k, e],
            recv_sem=halo_recv.at[k, e],
            device_id=beside[way],
            device_id_type=pl.DeviceIdType.MESH,
        )

    def halo_stage(k, values):
        for e in range(4):
            halo_out[k, e] = values[:, e * 128 : (e + 1) * 128]

    def halo_send_all(k, back):
        for e in range(4):
            halo_copy(k, e, e ^ back).start()
            unsent.append(lambda e=e: halo_copy(k, e, e ^ back).wait_send())

    def halo_start(k, values, back):
        halo_stage(k, values)
        halo_send_all(k, back)

    def halo_wait(k, back):
        got = []
        for e in range(4):
            halo_copy(k, e, e ^ back).wait_recv()
            got.append(jnp.where(has[e ^ back], halo_in[k, e], 0.0))
        return jnp.concatenate(got, 1)

    lane = lax.broadcasted_iota(jnp.int32, (16, 128), 1)
    left = lane < 64

    def pair_at(x, z):
        return pl.ds(x * 16 + z * 2, 2)

    def remote(src, dst, send, recv, peer):
        return pltpu.make_async_remote_copy(
            src_ref=src,
            dst_ref=dst,
            send_sem=send,
            recv_sem=recv,
            device_id=peer,
            device_id_type=pl.DeviceIdType.MESH,
        )

    def slot_at(y, z):
        return gx * 16 + z * 2 + y

    def plane_copy(k, flip, d, slot):
        at = gathered.at[k, pl.ds(slot, 1)]
        return remote(
            at, at, plane_send.at[k, flip, d], plane_recv.at[k, flip, d], plane_peer(flip, d)
        )

    def x_copy(k, d, dx, x):
        at = gathered.at[k, pair_at(x, lax.rem(gz - d + 8, 8))]
        return remote(at, at, x_send.at[k, d, dx], x_recv.at[k, d, dx], x_peer(dx))

    def col_copy(k, d, slot):
        return remote(
            parts.at[k, slot],
            others.at[k, d],
            col_send.at[k, d],
            col_recv.at[k, d],
            (i, lax.rem(j + d, 4)),
        )

    def gather_start(k, restricted):
        mine = slot_at(gy, gz)
        block = jnp.where(left, restricted[:16], restricted[16:])
        gathered[k, pl.ds(mine, 1)] = block.reshape(1, 16, 128)
        for d in (4, 3, 5, 2, 6, 1, 7, 0):
            for flip in (1, 0):
                if flip or d:
                    plane_copy(k, flip, d, mine).start()

        def drain(d, carry):
            plane_copy(k, 0, d, mine).wait_send()
            plane_copy(k, 1, d, mine).wait_send()
            return carry

        unsent.append(lambda: lax.fori_loop(1, 8, drain, 0))
        unsent.append(lambda: plane_copy(k, 1, 0, mine).wait_send())

    def gather_spread(k, work):
        plane_copy(k, 1, 0, slot_at(1 - gy, gz)).wait_recv()
        for dx in (2, 1, 3):
            x_copy(k, 0, dx, gx).start()

        def step(t, carry):
            d = jnp.where(lax.rem(t, 2) == 1, (t + 1) // 2, 8 - t // 2)
            z = lax.rem(gz - d + 8, 8)
            plane_copy(k, 0, d, slot_at(gy, z)).wait_recv()
            plane_copy(k, 1, d, slot_at(1 - gy, z)).wait_recv()
            for dx in (2, 1, 3):
                x_copy(k, d, dx, gx).start()
            work(t)
            return carry

        lax.fori_loop(1, 8, step, 0)

        def drain(d, carry):
            for dx in range(1, 4):
                x_copy(k, d, dx, gx).wait_send()
            return carry

        unsent.append(lambda: lax.fori_loop(0, 8, drain, 0))

    def coarse_group(k, x):
        for y in range(2):
            for zz in range(4):
                a = gathered[k, x * 16 + zz * 4 + y]
                b = gathered[k, x * 16 + zz * 4 + 2 + y]
                top = jnp.where(left, a, pltpu.roll(b, 64, 1))
                low = jnp.where(left, pltpu.roll(a, 64, 1), b)
                hi, lo = halves(jnp.concatenate([top, low], 0))
                at = pl.ds((y * 4 + zz) * 128, 128)
                x_hi[0:32, at] = hi
                x_hi[32:64, at] = lo
        at = pl.ds(pl.multiple_of(x * 1024, 1024), 1024)
        both = dot(x_hi[...], coarse_hi[:, at], NT)
        return both[:32] + both[32:] + dot(x_hi[0:32, :], coarse_lo[:, at], NT)

    def coarse_apply(k):
        part = coarse_group(k, gx)
        for dx in (1, 3, 2):
            x = lax.rem(gx - dx + 4, 4)

            def arrived(d, carry, dx=dx, x=x):
                x_copy(k, d, dx, x).wait_recv()
                return carry

            lax.fori_loop(0, 8, arrived, 0)
            part = part + coarse_group(k, x)
        for c in range(4):
            a = part[:16, (c // 2) * 128 : (c // 2) * 128 + 128]
            b = part[16:, (c // 2) * 128 : (c // 2) * 128 + 128]
            if c % 2 == 0:
                packed = jnp.where(left, a, pltpu.roll(b, 64, 1))
            else:
                packed = jnp.where(left, pltpu.roll(a, 64, 1), b)
            parts[k, c] = packed
        for d in (2, 1, 3):
            col_copy(k, d, lax.rem(j + d, 4)).start()
            unsent.append(lambda d=d: col_copy(k, d, lax.rem(j + d, 4)).wait_send())

    def coarse_finish(k):
        total = parts[k, j]
        for d in (1, 3, 2):
            col_copy(k, d, lax.rem(j + d, 4)).wait_recv()
            total = total + others[k, d]
        zero = jnp.zeros_like(total)
        return jnp.concatenate([jnp.where(left, total, zero), jnp.where(left, zero, total)], 0)

    def restrict(own, cols):
        return dot_thrice(own, modes_hi[:, cols], modes_lo[:, cols], NT)

    own_cols = slice(0, 512)
    rim_cols = slice(512, 1024)

    def pick(field):
        return dot_twice(field, pick_mat[...], NN)

    def scatter(bands):
        return dot_twice(bands, pick_t[...], NN)

    def stiff_prepare():
        loads[4].wait()
        loads[5].wait()

        def turn(t, carry):
            at = pl.ds(pl.multiple_of(t * 128, 128), 128)
            idx = jnp.concatenate([index_raw[:, at], jnp.zeros((48, 128), jnp.int32)], 0).T
            val = jnp.concatenate([coef_raw[:, at], jnp.zeros((48, 128), F32)], 0).T
            low_t[at, :] = (idx & 127).astype(F32)
            high_t[at, :] = (idx >> 7).astype(F32)
            hi = val.astype(BF).astype(F32)
            coef_hi[at, :] = hi
            coef_lo[at, :] = val - hi
            return carry

        lax.fori_loop(0, 8, turn, 0)

    def stiff_build(begin, end):
        lanes = lax.broadcasted_iota(jnp.int32, (128, 128), 0).astype(F32).astype(BF)
        blocks = lax.broadcasted_iota(jnp.int32, (8, 128), 0).astype(F32)
        one = jnp.ones((128, 128), BF)
        none = jnp.zeros((128, 128), BF)
        blank = jnp.zeros((16, 128), BF)

        def some(g, carry):
            for q in range(UNROLL // 4):
                hot = []
                val = []
                s = g * UNROLL + q * 4
                for r in range(4):
                    at = pl.ds(s + r, 1)
                    low = jnp.broadcast_to(low_t[at, :], (128, 128)).astype(BF)
                    hot.append(jnp.where(low == lanes, one, none))
                    hit = jnp.broadcast_to(high_t[at, :], (8, 128)) == blocks
                    pair = [jnp.where(hit, coef_hi[at, :], 0.0), jnp.where(hit, coef_lo[at, :], 0.0)]
                    val.append(jnp.concatenate(pair, 0).astype(BF))
                right = jnp.concatenate(
                    [jnp.concatenate(hot[:2], 1), jnp.concatenate(hot[2:], 1)], 0
                )
                rows = [
                    jnp.concatenate([val[r], blank] if r % 2 == 0 else [blank, val[r]], 1)
                    for r in range(4)
                ]
                out = dot(jnp.concatenate(rows, 0), right, NT)
                for r in range(4):
                    cut = out[16 * r : 16 * r + 16, (r // 2) * 128 : (r // 2) * 128 + 128]
                    tiles[pl.ds(pl.multiple_of((s + r) * 8, 8), 8), :] = cut[:8] + cut[8:]
            return carry

        if begin is end:
            some(begin, 0)
        else:
            lax.fori_loop(begin, end, some, 0)

    def stiff_finish():
        for r in range(4):
            for c in range(8):
                hi, lo = halves(tiles[pl.ds(c + r * 2048, 256, stride=8), :])
                stiff_hi[r * 256 : r * 256 + 256, c * 128 : c * 128 + 128] = hi
                stiff_lo[r * 256 : r * 256 + 256, c * 128 : c * 128 + 128] = lo

    def local_solve(resid, rim):
        local_buf[...] = dot_thrice(jnp.concatenate([resid, rim], 1), inv_hi[...], inv_lo[...], NT)

    def spread_cols(spread, cols):
        return local_buf[:, cols] + dot_thrice(spread, modes_hi[:, cols], modes_lo[:, cols], NN)

    def start_fold(k, fold_k, spread):
        halo_start(fold_k, spread_cols(spread, rim_cols), 1)
        return spread_cols(spread, own_cols)

    def nothing(*unused):
        return None

    loads[1].wait()
    rhs = rhs_ref[...]
    halo_stage(0, pick(rhs))
    stiff_prepare()
    stiff_build(0, 4)
    pl.semaphore_wait(barrier, len(greet))
    halo_send_all(0, 0)

    loads[2].wait()
    m_hi, m_lo = halves(modes_raw[...])
    modes_hi[...] = jnp.concatenate([m_hi, m_hi], 0)
    modes_lo[...] = jnp.concatenate([m_lo, m_lo], 0)
    pick_t[...] = pick_mat[...].astype(F32).T.astype(BF)
    gram[...] = dot(pick_t[...], pick_mat[...], NN).astype(BF)
    stiff_build(4, 9)
    restricted = restrict(rhs, own_cols)
    rim = halo_wait(0, 0)
    def stiff_step(t):
        at = 8 + t
        stiff_build(at, at)

    gather_start(0, restricted + restrict(rim, rim_cols))
    loads[6].wait()
    split_into(inv_raw, inv_hi, inv_lo, 1024, 128)
    local_solve(rhs, rim)
    gather_spread(0, stiff_step)
    loads[7].wait()
    split_into(coarse_raw, coarse_hi, coarse_lo, 256, 32)
    coarse_apply(0)
    stiff_finish()
    spread = coarse_finish(0)
    own = start_fold(0, 1, spread)
    picked = pick(own)
    back = halo_wait(1, 1)
    halo_start(2, picked + dot_twice(back, gram[...], NN), 0)
    first = own + scatter(back)
    first_buf[...] = first

    part = dot_thrice(first, stiff_hi[:, own_cols], stiff_lo[:, own_cols], NT)
    loads[3].wait()
    diag = diag_ref[...]
    rim = halo_wait(2, 0)
    bands = part[:, rim_cols] + diag[:, rim_cols] * rim + dot_thrice(
        rim, stiff_hi[rim_cols, rim_cols], stiff_lo[rim_cols, rim_cols], NT
    )
    halo_start(3, bands, 1)
    own = part[:, own_cols] + diag[:, own_cols] * first + dot_thrice(
        rim, stiff_hi[own_cols, rim_cols], stiff_lo[own_cols, rim_cols], NT
    )
    own = rhs - own
    picked = pick(own)
    back = halo_wait(3, 1)
    halo_start(4, picked - dot_twice(back, gram[...], NN), 0)
    residual = own - scatter(back)
    res_buf[...] = residual
    res_copy = pltpu.make_async_copy(res_buf, res_hbm, load_sem.at[8])
    res_copy.start()

    restricted = restrict(residual, own_cols)
    rim = halo_wait(4, 0)
    gather_start(1, restricted + restrict(rim, rim_cols))
    local_solve(residual, rim)
    gather_spread(1, nothing)
    coarse_apply(1)
    spread = coarse_finish(1)
    own = first_buf[...] + start_fold(1, 5, spread)
    back = halo_wait(5, 1)
    first_buf[...] = own + scatter(back)
    sol_copy = pltpu.make_async_copy(first_buf, sol_hbm, load_sem.at[9])
    sol_copy.start()
    for finish in unsent:
        finish()
    res_copy.wait()
    sol_copy.wait()


def body(
    right_side, local_inverse, modes, coarse_inverse, stiff_diag, nbr_index, nbr_coef, send_rows
):
    hbm = pl.BlockSpec(memory_space=pltpu.HBM)
    field = jax.ShapeDtypeStruct((32, 512), F32)
    dma = pltpu.SemaphoreType.DMA
    scratch = [
        pltpu.VMEM((32, 512), F32),
        pltpu.VMEM((1, 1024), F32),
        pltpu.VMEM((4, 128), jnp.int32),
        pltpu.VMEM((1024, 1024), F32),
        pltpu.VMEM((256, 4096), F32),
        pltpu.VMEM((64, 1024), F32),
        pltpu.VMEM((80, 1024), jnp.int32),
        pltpu.VMEM((80, 1024), F32),
        pltpu.VMEM((1024, 1024), BF),
        pltpu.VMEM((1024, 1024), BF),
        pltpu.VMEM((256, 4096), BF),
        pltpu.VMEM((256, 4096), BF),
        pltpu.VMEM((128, 1024), BF),
        pltpu.VMEM((128, 1024), BF),
        pltpu.VMEM((512, 512), BF),
        pltpu.VMEM((512, 512), BF),
        pltpu.VMEM((512, 512), BF),
        pltpu.VMEM((32, 512), F32),
        pltpu.VMEM((1024, 128), F32),
        pltpu.VMEM((1024, 128), F32),
        pltpu.VMEM((1024, 128), F32),
        pltpu.VMEM((1024, 128), F32),
        pltpu.VMEM((8192, 128), F32),
        pltpu.VMEM((1024, 1024), BF),
        pltpu.VMEM((1024, 1024), BF),
        pltpu.VMEM((64, 1024), BF),
        pltpu.VMEM((6, 4, 32, 128), F32),
        pltpu.VMEM((6, 4, 32, 128), F32),
        pltpu.VMEM((2, 64, 16, 128), F32),
        pltpu.VMEM((2, 4, 16, 128), F32),
        pltpu.VMEM((2, 4, 16, 128), F32),
        pltpu.VMEM((32, 1024), F32),
        pltpu.VMEM((32, 512), F32),
        dma((10,)),
        dma((6, 4)),
        dma((6, 4)),
        dma((2, 2, 8)),
        dma((2, 2, 8)),
        dma((2, 8, 4)),
        dma((2, 8, 4)),
        dma((2, 4)),
        dma((2, 4)),
    ]
    return tuple(
        pl.pallas_call(
            kernel,
            out_shape=(field, field),
            in_specs=[hbm] * 8,
            out_specs=(hbm, hbm),
            scratch_shapes=scratch,
            compiler_params=pltpu.CompilerParams(
                collective_id=0, has_side_effects=True, vmem_limit_bytes=60 * 2**20
            ),
            name="schwarz",
        )(
            right_side,
            local_inverse[0, 0],
            modes[0, 0],
            coarse_inverse,
            stiff_diag[0],
            nbr_index[0, 0],
            nbr_coef[0, 0],
            send_rows[0, 0],
        )
    )


def solution(mesh):
    in_specs = (
        P(None, ("rows", "cols")),
        P("rows", "cols", None, None),
        P("rows", "cols", None, None),
        P("rows", "cols"),
        P("rows", "cols", None),
        P("rows", "cols", None, None),
        P("rows", "cols", None, None),
        P("rows", "cols", None, None),
    )
    out_specs = (P(None, ("rows", "cols")), P(None, ("rows", "cols")))
    return jax.shard_map(body, mesh=mesh, in_specs=in_specs, out_specs=out_specs, check_vma=False)
```

time: 94.6 us -> 81 us (0.86)
  Pallas kernels: 84.9 us -> 77.1 us
  local copies, waits for them, and re-layouts: 8.54 us -> 2.95 us
    pallas_call x1, Pallas kernels: 84.9 us -> 77.1 us  [body(): pl.pallas_call(kernel, out_shape=(field, field), in_specs=[hbm] * 8, out_...]
    unnamed x16 -> x2, local copies, waits for them, and re-layouts: 8.54 us -> 2.95 us
where the time goes in v2:
time: 81 us; the launch traced here: 80.7 us
  Pallas kernels  77.1 us (95%)
  local copies, waits for them, and re-layouts  2.95 us (4%)
    pallas_call x1, Pallas kernels, body(): pl.pallas_call(kernel, out_shape=(field, field), in_specs=[hbm] * 8, out_...  77.1 us
    unnamed x2, local copies, waits for them, and re-layouts  2.95 us

profile of v2, /device:TPU:1, one launch (start us, length us, event | category | flops | bytes accessed | tf_op | source)
XLA Modules:
  0.0 80.7 jit_solution(8351692018096426707)
XLA Ops:
  0.6 77.1 %schwarz.1 = (f32[32,512]{1,0:T(8,128)}, f32[32,512]{1,0:T(8,128)}) custom-call(f32[32,512]{1,0:T(8,128)} %rhs_hbm.1, f32[1024,1024]{1,0:T(8,128)} %bitcast.6, f32[64,1024]{1,0:T(8,128)} %bitcast.9, f32[256,4096]{1,0:T(8,128)} %coarse_hbm.1, f32[1,1024]{1,0:T(1,128)} %bitcast.10, s32[80,1024]{1,0:T(8,128)} %bitcast.7, f32[80,1024]{1,0:T(8,128)} %bitcast.8, ...), custom_call_target="tpu_custom_call" | custom-call | tf_op jit(solution)/shard_map/schwarz/pallas_call | solution.py:482
  77.8 1.5 %copy.12 = f32[32,512]{1,0:T(8,128)} copy(f32[32,512]{1,0:T(8,128)} %get-tuple-element.4) | data formatting | bytes 131072
  79.2 1.5 %copy.13 = f32[32,512]{1,0:T(8,128)} copy(f32[32,512]{1,0:T(8,128)} %get-tuple-element.5) | data formatting | bytes 131072

commit v3 on v2

--- a/solution.py
+++ b/solution.py
@@ -52,9 +52,9 @@
     rhs_ref, diag_ref, sends_ref, inv_raw, coarse_raw, modes_raw, index_raw, coef_raw,
     inv_hi, inv_lo, coarse_hi, coarse_lo, modes_hi, modes_lo,
     pick_mat, pick_t, gram, res_buf, low_t, high_t, coef_hi, coef_lo, tiles, stiff_hi, stiff_lo,
-    x_hi, halo_out, halo_in, gathered, parts, others, local_buf, first_buf,
+    x_hi, own_buf, lent_buf, folded_hi, folded_lo, lent_hi, lent_lo, basis_in, near, halo_out, halo_in, gathered, parts, others, local_buf, first_buf,
     load_sem, halo_send, halo_recv, plane_send, plane_recv, x_send, x_recv,
-    col_send, col_recv,
+    col_send, col_recv, row_send, row_recv, basis_send, basis_recv,
 ):
     i = lax.axis_index("rows")
     j = lax.axis_index("cols")
@@ -99,7 +99,8 @@
     unsent = []
     barrier = pltpu.get_barrier_semaphore()
     greet = [plane_peer(flip, d) for d in (4, 3, 5, 2, 6, 1, 7, 0) for flip in (1, 0) if flip or d]
-    greet = greet + [x_peer(d) for d in (2, 1, 3)] + beside + [(i, lax.rem(j + 2, 4))]
+    greet = greet + [x_peer(d) for d in (2, 1, 3)] + [(i, lax.rem(j + d, 4)) for d in (2, 1, 3)]
+    greet = greet + [(lax.rem(i + way, 64), lax.rem(j + d, 4)) for way in (1, 63) for d in range(4)]
     for peer in greet:
         pl.semaphore_signal(barrier, inc=1, device_id=peer, device_id_type=pl.DeviceIdType.MESH)
 
@@ -170,13 +171,32 @@
         at = gathered.at[k, pair_at(x, lax.rem(gz - d + 8, 8))]
         return remote(at, at, x_send.at[k, d, dx], x_recv.at[k, d, dx], x_peer(dx))
 
-    def col_copy(k, d, slot):
+    def col_copy(k, d):
         return remote(
-            parts.at[k, slot],
+            parts.at[k],
             others.at[k, d],
             col_send.at[k, d],
             col_recv.at[k, d],
             (i, lax.rem(j + d, 4)),
+        )
+
+    def row_copy(k, way, d):
+        col = lax.rem(j + d, 4)
+        return remote(
+            parts.at[k, col],
+            near.at[k, way, d],
+            row_send.at[k, way, d],
+            row_recv.at[k, way, d],
+            (lax.rem(i + (1, 63)[way], 64), col),
+        )
+
+    def basis_copy(e):
+        return remote(
+            modes_raw.at[:, pl.ds(512 + e * 128, 128)],
+            basis_in.at[e],
+            basis_send.at[e],
+            basis_recv.at[e],
+            beside[e ^ 1],
         )
 
     def gather_start(k, restricted):
@@ -254,17 +274,39 @@
             else:
                 packed = jnp.where(left, pltpu.roll(a, 64, 1), b)
             parts[k, c] = packed
+        for d in range(4):
+            for way in range(2):
+                row_copy(k, way, d).start()
+                unsent.append(lambda way=way, d=d: row_copy(k, way, d).wait_send())
         for d in (2, 1, 3):
-            col_copy(k, d, lax.rem(j + d, 4)).start()
-            unsent.append(lambda d=d: col_copy(k, d, lax.rem(j + d, 4)).wait_send())
+            col_copy(k, d).start()
+            unsent.append(lambda d=d: col_copy(k, d).wait_send())
 
     def coarse_finish(k):
-        total = parts[k, j]
         for d in (1, 3, 2):
-            col_copy(k, d, lax.rem(j + d, 4)).wait_recv()
-            total = total + others[k, d]
-        zero = jnp.zeros_like(total)
-        return jnp.concatenate([jnp.where(left, total, zero), jnp.where(left, zero, total)], 0)
+            col_copy(k, d).wait_recv()
+        for d in range(4):
+            for way in range(2):
+                row_copy(k, way, d).wait_recv()
+
+        def in_row(col):
+            return parts[k, col] + others[k, 1, col] + others[k, 2, col] + others[k, 3, col]
+
+        def in_near(way):
+            return near[k, way, 0] + near[k, way, 1] + near[k, way, 2] + near[k, way, 3]
+
+        sums = [
+            in_row(j),
+            jnp.where(has[1], in_near(1), 0.0),
+            jnp.where(has[0], in_near(0), 0.0),
+            jnp.where(has[3], in_row(lax.rem(j + 1, 4)), 0.0),
+            jnp.where(has[2], in_row(lax.rem(j + 3, 4)), 0.0),
+        ]
+        zero = jnp.zeros((16, 128), F32)
+        rows = [
+            jnp.concatenate([jnp.where(left, t, zero), jnp.where(left, zero, t)], 0) for t in sums
+        ]
+        return jnp.concatenate(rows, 1)
 
     def restrict(own, cols):
         return dot_thrice(own, modes_hi[:, cols], modes_lo[:, cols], NT)
@@ -342,12 +384,25 @@
     def local_solve(resid, rim):
         local_buf[...] = dot_thrice(jnp.concatenate([resid, rim], 1), inv_hi[...], inv_lo[...], NT)
 
-    def spread_cols(spread, cols):
-        return local_buf[:, cols] + dot_thrice(spread, modes_hi[:, cols], modes_lo[:, cols], NN)
-
-    def start_fold(k, fold_k, spread):
-        halo_start(fold_k, spread_cols(spread, rim_cols), 1)
-        return spread_cols(spread, own_cols)
+    def fold_basis():
+        folded_hi[0:128, :] = modes_hi[:, own_cols]
+        folded_lo[0:128, :] = modes_lo[:, own_cols]
+        for e in range(4):
+            basis_copy(e).wait_recv()
+            field = dot_twice(basis_in[e], pick_t[e * 128 : (e + 1) * 128, :], NN)
+            hi, lo = halves(field)
+            at = slice(128 + e * 128, 256 + e * 128)
+            folded_hi[at, :] = jnp.concatenate([hi, hi], 0)
+            folded_lo[at, :] = jnp.concatenate([lo, lo], 0)
+        lent_hi[...] = dot(folded_hi[...], pick_mat[...], NN).astype(BF)
+        lent_lo[...] = dot(folded_lo[...], pick_mat[...], NN).astype(BF)
+
+    def local_start(fold_k, resid, rim):
+        local_solve(resid, rim)
+        halo_start(fold_k, local_buf[:, rim_cols], 1)
+
+    def local_finish(fold_k):
+        own_buf[...] = local_buf[:, own_cols] + scatter(halo_wait(fold_k, 1))
 
     def nothing(*unused):
         return None
@@ -359,8 +414,11 @@
     stiff_build(0, 4)
     pl.semaphore_wait(barrier, len(greet))
     halo_send_all(0, 0)
-
     loads[2].wait()
+    for e in range(4):
+        basis_copy(e).start()
+        unsent.append(lambda e=e: basis_copy(e).wait_send())
+
     m_hi, m_lo = halves(modes_raw[...])
     modes_hi[...] = jnp.concatenate([m_hi, m_hi], 0)
     modes_lo[...] = jnp.concatenate([m_lo, m_lo], 0)
@@ -370,24 +428,27 @@
     restricted = restrict(rhs, own_cols)
     rim = halo_wait(0, 0)
     def stiff_step(t):
-        at = 8 + t
-        stiff_build(at, at)
+        @pl.when(t < 4)
+        def _():
+            at = 8 + t
+            stiff_build(at, at)
 
     gather_start(0, restricted + restrict(rim, rim_cols))
     loads[6].wait()
     split_into(inv_raw, inv_hi, inv_lo, 1024, 128)
-    local_solve(rhs, rim)
+    local_start(1, rhs, rim)
     gather_spread(0, stiff_step)
     loads[7].wait()
     split_into(coarse_raw, coarse_hi, coarse_lo, 256, 32)
+    fold_basis()
     coarse_apply(0)
+    local_finish(1)
+    lent_buf[...] = pick(own_buf[...])
+    stiff_build(12, 16)
     stiff_finish()
     spread = coarse_finish(0)
-    own = start_fold(0, 1, spread)
-    picked = pick(own)
-    back = halo_wait(1, 1)
-    halo_start(2, picked + dot_twice(back, gram[...], NN), 0)
-    first = own + scatter(back)
+    halo_start(2, lent_buf[...] + dot_thrice(spread, lent_hi[...], lent_lo[...], NN), 0)
+    first = own_buf[...] + dot_thrice(spread, folded_hi[...], folded_lo[...], NN)
     first_buf[...] = first
 
     part = dot_thrice(first, stiff_hi[:, own_cols], stiff_lo[:, own_cols], NT)
@@ -409,23 +470,34 @@
     res_buf[...] = residual
     res_copy = pltpu.make_async_copy(res_buf, res_hbm, load_sem.at[8])
     res_copy.start()
+    unsent.append(res_copy.wait)
 
     restricted = restrict(residual, own_cols)
     rim = halo_wait(4, 0)
     gather_start(1, restricted + restrict(rim, rim_cols))
-    local_solve(residual, rim)
+    local_start(5, residual, rim)
     gather_spread(1, nothing)
     coarse_apply(1)
+    local_finish(5)
+    base = first_buf[...] + own_buf[...]
     spread = coarse_finish(1)
-    own = first_buf[...] + start_fold(1, 5, spread)
-    back = halo_wait(5, 1)
-    first_buf[...] = own + scatter(back)
+    first_buf[...] = base + dot_thrice(spread, folded_hi[...], folded_lo[...], NN)
     sol_copy = pltpu.make_async_copy(first_buf, sol_hbm, load_sem.at[9])
     sol_copy.start()
     for finish in unsent:
         finish()
-    res_copy.wait()
     sol_copy.wait()
+
+
+def hand_on(sol_in, res_in, sol_out, res_out, sems):
+    copies = [
+        pltpu.make_async_copy(sol_in, sol_out, sems.at[0]),
+        pltpu.make_async_copy(res_in, res_out, sems.at[1]),
+    ]
+    for copy in copies:
+        copy.start()
+    for copy in copies:
+        copy.wait()
 
 
 def body(
@@ -461,11 +533,19 @@
         pltpu.VMEM((1024, 1024), BF),
         pltpu.VMEM((1024, 1024), BF),
         pltpu.VMEM((64, 1024), BF),
+        pltpu.VMEM((32, 512), F32),
+        pltpu.VMEM((32, 512), F32),
+        pltpu.VMEM((640, 512), BF),
+        pltpu.VMEM((640, 512), BF),
+        pltpu.VMEM((640, 512), BF),
+        pltpu.VMEM((640, 512), BF),
+        pltpu.VMEM((4, 64, 128), F32),
+        pltpu.VMEM((2, 2, 4, 16, 128), F32),
         pltpu.VMEM((6, 4, 32, 128), F32),
         pltpu.VMEM((6, 4, 32, 128), F32),
         pltpu.VMEM((2, 64, 16, 128), F32),
         pltpu.VMEM((2, 4, 16, 128), F32),
-        pltpu.VMEM((2, 4, 16, 128), F32),
+        pltpu.VMEM((2, 4, 4, 16, 128), F32),
         pltpu.VMEM((32, 1024), F32),
         pltpu.VMEM((32, 512), F32),
         dma((10,)),
@@ -477,8 +557,12 @@
         dma((2, 8, 4)),
         dma((2, 4)),
         dma((2, 4)),
+        dma((2, 2, 4)),
+        dma((2, 2, 4)),
+        dma((4,)),
+        dma((4,)),
     ]
-    return tuple(
+    results = tuple(
         pl.pallas_call(
             kernel,
             out_shape=(field, field),
@@ -500,6 +584,16 @@
             send_rows[0, 0],
         )
     )
+    return tuple(
+        pl.pallas_call(
+            hand_on,
+            out_shape=(field, field),
+            in_specs=[hbm] * 2,
+            out_specs=(hbm, hbm),
+            scratch_shapes=[dma((2,))],
+            name="results",
+        )(*results)
+    )
 
 
 def solution(mesh):

time: 81 us -> 77.8 us (0.960)
  local copies, waits for them, and re-layouts: 2.95 us -> 0 us
    pallas_call x1, Pallas kernels: 77.1 us -> 72 us  [body(): pl.pallas_call(kernel, out_shape=(field, field), in_specs=[hbm] * 8, out_...]
    pallas_call x0 -> x1, Pallas kernels: none -> 5.09 us  [body(): pl.pallas_call(hand_on, out_shape=(field, field), in_specs=[hbm] * 2, out...]
    unnamed x2 -> x0, local copies, waits for them, and re-layouts: 2.95 us -> none
where the time goes in v3:
time: 77.8 us; the launch traced here: 77.7 us
  Pallas kernels  77.1 us (99%)
    pallas_call x1, Pallas kernels, body(): pl.pallas_call(kernel, out_shape=(field, field), in_specs=[hbm] * 8, out_...  72 us
    pallas_call x1, Pallas kernels, body(): pl.pallas_call(hand_on, out_shape=(field, field), in_specs=[hbm] * 2, out...  5.09 us

profile of v3, /device:TPU:1, one launch (start us, length us, event | category | flops | bytes accessed | tf_op | source)
XLA Modules:
  0.0 77.7 jit_solution(16123252277125304838)
XLA Ops:
  0.6 72.0 %schwarz.1 = (f32[32,512]{1,0:T(8,128)}, f32[32,512]{1,0:T(8,128)}) custom-call(f32[32,512]{1,0:T(8,128)} %rhs_hbm.1, f32[1024,1024]{1,0:T(8,128)} %bitcast.6, f32[64,1024]{1,0:T(8,128)} %bitcast.9, f32[256,4096]{1,0:T(8,128)} %coarse_hbm.1, f32[1,1024]{1,0:T(1,128)} %bitcast.10, s32[80,1024]{1,0:T(8,128)} %bitcast.7, f32[80,1024]{1,0:T(8,128)} %bitcast.8, ...), custom_call_target="tpu_custom_call" | custom-call | tf_op jit(solution)/shard_map/schwarz/pallas_call | solution.py:566
  72.6 5.1 %results.1 = (f32[32,512]{1,0:T(8,128)}, f32[32,512]{1,0:T(8,128)}) custom-call(f32[32,512]{1,0:T(8,128)} %get-tuple-element.4.sol_in, f32[32,512]{1,0:T(8,128)} %get-tuple-element.5.res_in), custom_call_target="tpu_custom_call" | custom-call | tf_op jit(solution)/shard_map/results/pallas_call | solution.py:588

commit v4 on v3

--- a/solution.py
+++ b/solution.py
@@ -9,7 +9,7 @@
 F32 = jnp.float32
 NT = (((1,), (1,)), ((), ()))
 NN = (((1,), (0,)), ((), ()))
-UNROLL = 64
+UNROLL = 32
 
 
 def dot(a, b, dims):
@@ -48,10 +48,10 @@
 
 def kernel(
     rhs_hbm, inv_hbm, modes_hbm, coarse_hbm, diag_hbm, index_hbm, coef_hbm, sends_hbm,
-    sol_hbm, res_hbm,
+    sol_ref, res_ref,
     rhs_ref, diag_ref, sends_ref, inv_raw, coarse_raw, modes_raw, index_raw, coef_raw,
     inv_hi, inv_lo, coarse_hi, coarse_lo, modes_hi, modes_lo,
-    pick_mat, pick_t, gram, res_buf, low_t, high_t, coef_hi, coef_lo, tiles, stiff_hi, stiff_lo,
+    pick_mat, pick_t, gram, low_t, high_t, coef_hi, coef_lo, tiles, stiff_hi, stiff_lo,
     x_hi, own_buf, lent_buf, folded_hi, folded_lo, lent_hi, lent_lo, basis_in, near, halo_out, halo_in, gathered, parts, others, local_buf, first_buf,
     load_sem, halo_send, halo_recv, plane_send, plane_recv, x_send, x_recv,
     col_send, col_recv, row_send, row_recv, basis_send, basis_recv,
@@ -324,49 +324,54 @@
         loads[4].wait()
         loads[5].wait()
 
-        def turn(t, carry):
-            at = pl.ds(pl.multiple_of(t * 128, 128), 128)
-            idx = jnp.concatenate([index_raw[:, at], jnp.zeros((48, 128), jnp.int32)], 0).T
-            val = jnp.concatenate([coef_raw[:, at], jnp.zeros((48, 128), F32)], 0).T
+        for t in range(3):
+            def stack(raw, dtype):
+                rows = [
+                    raw[:, p * 384 + t * 128 : p * 384 + t * 128 + 128]
+                    if p * 384 + t * 128 < 1024
+                    else jnp.zeros((80, 128), dtype)
+                    for p in range(3)
+                ]
+                rows.append(jnp.zeros((16, 128), dtype))
+                return jnp.concatenate(rows, 0).T
+
+            at = slice(t * 128, t * 128 + 128)
+            idx = stack(index_raw, jnp.int32)
+            val = stack(coef_raw, F32)
             low_t[at, :] = (idx & 127).astype(F32)
             high_t[at, :] = (idx >> 7).astype(F32)
             hi = val.astype(BF).astype(F32)
             coef_hi[at, :] = hi
             coef_lo[at, :] = val - hi
-            return carry
-
-        lax.fori_loop(0, 8, turn, 0)
 
     def stiff_build(begin, end):
-        lanes = lax.broadcasted_iota(jnp.int32, (128, 128), 0).astype(F32).astype(BF)
-        blocks = lax.broadcasted_iota(jnp.int32, (8, 128), 0).astype(F32)
-        one = jnp.ones((128, 128), BF)
-        none = jnp.zeros((128, 128), BF)
-        blank = jnp.zeros((16, 128), BF)
+        lanes = lax.broadcasted_iota(jnp.int32, (128, 256), 0).astype(F32).astype(BF)
+        blocks = lax.broadcasted_iota(jnp.int32, (8, 256), 0).astype(F32)
+        one = jnp.ones((128, 256), BF)
+        none = jnp.zeros((128, 256), BF)
+        third = lax.broadcasted_iota(jnp.int32, (8, 256), 1) // 80
 
         def some(g, carry):
-            for q in range(UNROLL // 4):
+            for q in range(UNROLL // 2):
                 hot = []
                 val = []
-                s = g * UNROLL + q * 4
-                for r in range(4):
+                s = g * UNROLL + q * 2
+                for r in range(2):
                     at = pl.ds(s + r, 1)
-                    low = jnp.broadcast_to(low_t[at, :], (128, 128)).astype(BF)
+                    low = jnp.broadcast_to(low_t[at, :], (128, 256)).astype(BF)
                     hot.append(jnp.where(low == lanes, one, none))
-                    hit = jnp.broadcast_to(high_t[at, :], (8, 128)) == blocks
-                    pair = [jnp.where(hit, coef_hi[at, :], 0.0), jnp.where(hit, coef_lo[at, :], 0.0)]
-                    val.append(jnp.concatenate(pair, 0).astype(BF))
-                right = jnp.concatenate(
-                    [jnp.concatenate(hot[:2], 1), jnp.concatenate(hot[2:], 1)], 0
-                )
-                rows = [
-                    jnp.concatenate([val[r], blank] if r % 2 == 0 else [blank, val[r]], 1)
-                    for r in range(4)
-                ]
-                out = dot(jnp.concatenate(rows, 0), right, NT)
-                for r in range(4):
-                    cut = out[16 * r : 16 * r + 16, (r // 2) * 128 : (r // 2) * 128 + 128]
-                    tiles[pl.ds(pl.multiple_of((s + r) * 8, 8), 8), :] = cut[:8] + cut[8:]
+                    hit = jnp.broadcast_to(high_t[at, :], (8, 256)) == blocks
+                    high = jnp.where(hit, coef_hi[at, :], 0.0)
+                    rest = jnp.where(hit, coef_lo[at, :], 0.0)
+                    for p in range(3):
+                        pair = [jnp.where(third == p, high, 0.0), jnp.where(third == p, rest, 0.0)]
+                        val.append(jnp.concatenate(pair, 0).astype(BF))
+                out = dot(jnp.concatenate(val, 0), jnp.concatenate(hot, 0), NT)
+                for r in range(2):
+                    for p in range(3):
+                        cut = out[(r * 3 + p) * 16 : (r * 3 + p) * 16 + 16, r * 128 : r * 128 + 128]
+                        row = (p * 384 + s + r) * 8
+                        tiles[pl.ds(pl.multiple_of(row, 8), 8), :] = cut[:8] + cut[8:]
             return carry
 
         if begin is end:
@@ -422,15 +427,24 @@
     m_hi, m_lo = halves(modes_raw[...])
     modes_hi[...] = jnp.concatenate([m_hi, m_hi], 0)
     modes_lo[...] = jnp.concatenate([m_lo, m_lo], 0)
-    pick_t[...] = pick_mat[...].astype(F32).T.astype(BF)
-    gram[...] = dot(pick_t[...], pick_mat[...], NN).astype(BF)
-    stiff_build(4, 9)
+    columns = jnp.concatenate([sends_ref[...], sends_ref[...]], 0).T
+    lane_ids = lax.broadcasted_iota(jnp.int32, (128, 512), 1)
+    for e in range(4):
+        column = columns[:, e : e + 1]
+        at = slice(e * 128, e * 128 + 128)
+        hit = jnp.broadcast_to(column, (128, 512)) == lane_ids
+        pick_t[at, :] = jnp.where(hit, 1.0, 0.0).astype(BF)
+        for f in range(4):
+            row = jnp.broadcast_to(sends_ref[f : f + 1, :], (128, 128))
+            hit = jnp.broadcast_to(column, (128, 128)) == row
+            gram[at, f * 128 : f * 128 + 128] = jnp.where(hit, 1.0, 0.0).astype(BF)
+    stiff_build(4, 8)
     restricted = restrict(rhs, own_cols)
     rim = halo_wait(0, 0)
     def stiff_step(t):
-        @pl.when(t < 4)
+        @pl.when(t == 1)
         def _():
-            at = 8 + t
+            at = 7 + t
             stiff_build(at, at)
 
     gather_start(0, restricted + restrict(rim, rim_cols))
@@ -444,7 +458,7 @@
     coarse_apply(0)
     local_finish(1)
     lent_buf[...] = pick(own_buf[...])
-    stiff_build(12, 16)
+    stiff_build(9, 12)
     stiff_finish()
     spread = coarse_finish(0)
     halo_start(2, lent_buf[...] + dot_thrice(spread, lent_hi[...], lent_lo[...], NN), 0)
@@ -467,10 +481,7 @@
     back = halo_wait(3, 1)
     halo_start(4, picked - dot_twice(back, gram[...], NN), 0)
     residual = own - scatter(back)
-    res_buf[...] = residual
-    res_copy = pltpu.make_async_copy(res_buf, res_hbm, load_sem.at[8])
-    res_copy.start()
-    unsent.append(res_copy.wait)
+    res_ref[...] = residual
 
     restricted = restrict(residual, own_cols)
     rim = halo_wait(4, 0)
@@ -481,30 +492,17 @@
     local_finish(5)
     base = first_buf[...] + own_buf[...]
     spread = coarse_finish(1)
-    first_buf[...] = base + dot_thrice(spread, folded_hi[...], folded_lo[...], NN)
-    sol_copy = pltpu.make_async_copy(first_buf, sol_hbm, load_sem.at[9])
-    sol_copy.start()
+    sol_ref[...] = base + dot_thrice(spread, folded_hi[...], folded_lo[...], NN)
     for finish in unsent:
         finish()
-    sol_copy.wait()
-
-
-def hand_on(sol_in, res_in, sol_out, res_out, sems):
-    copies = [
-        pltpu.make_async_copy(sol_in, sol_out, sems.at[0]),
-        pltpu.make_async_copy(res_in, res_out, sems.at[1]),
-    ]
-    for copy in copies:
-        copy.start()
-    for copy in copies:
-        copy.wait()
 
 
 def body(
     right_side, local_inverse, modes, coarse_inverse, stiff_diag, nbr_index, nbr_coef, send_rows
 ):
     hbm = pl.BlockSpec(memory_space=pltpu.HBM)
-    field = jax.ShapeDtypeStruct((32, 512), F32)
+    field = pltpu.VMEM((32, 512), F32)
+    vmem = pl.BlockSpec(memory_space=pltpu.VMEM)
     dma = pltpu.SemaphoreType.DMA
     scratch = [
         pltpu.VMEM((32, 512), F32),
@@ -524,12 +522,11 @@
         pltpu.VMEM((512, 512), BF),
         pltpu.VMEM((512, 512), BF),
         pltpu.VMEM((512, 512), BF),
-        pltpu.VMEM((32, 512), F32),
-        pltpu.VMEM((1024, 128), F32),
-        pltpu.VMEM((1024, 128), F32),
-        pltpu.VMEM((1024, 128), F32),
-        pltpu.VMEM((1024, 128), F32),
-        pltpu.VMEM((8192, 128), F32),
+        pltpu.VMEM((384, 256), F32),
+        pltpu.VMEM((384, 256), F32),
+        pltpu.VMEM((384, 256), F32),
+        pltpu.VMEM((384, 256), F32),
+        pltpu.VMEM((9216, 128), F32),
         pltpu.VMEM((1024, 1024), BF),
         pltpu.VMEM((1024, 1024), BF),
         pltpu.VMEM((64, 1024), BF),
@@ -548,7 +545,7 @@
         pltpu.VMEM((2, 4, 4, 16, 128), F32),
         pltpu.VMEM((32, 1024), F32),
         pltpu.VMEM((32, 512), F32),
-        dma((10,)),
+        dma((8,)),
         dma((6, 4)),
         dma((6, 4)),
         dma((2, 2, 8)),
@@ -562,12 +559,12 @@
         dma((4,)),
         dma((4,)),
     ]
-    results = tuple(
+    return tuple(
         pl.pallas_call(
             kernel,
             out_shape=(field, field),
             in_specs=[hbm] * 8,
-            out_specs=(hbm, hbm),
+            out_specs=(vmem, vmem),
             scratch_shapes=scratch,
             compiler_params=pltpu.CompilerParams(
                 collective_id=0, has_side_effects=True, vmem_limit_bytes=60 * 2**20
@@ -584,16 +581,6 @@
             send_rows[0, 0],
         )
     )
-    return tuple(
-        pl.pallas_call(
-            hand_on,
-            out_shape=(field, field),
-            in_specs=[hbm] * 2,
-            out_specs=(hbm, hbm),
-            scratch_shapes=[dma((2,))],
-            name="results",
-        )(*results)
-    )
 
 
 def solution(mesh):

time: 77.8 us -> 73.4 us (0.943)
  Pallas kernels: 77.1 us -> 71.4 us
  local copies, waits for them, and re-layouts: 0 us -> 1.26 us
    pallas_call x1 -> x0, Pallas kernels: 5.09 us -> none  [body(): pl.pallas_call(hand_on, out_shape=(field, field), in_specs=[hbm] * 2, out...]
    unnamed x0 -> x2, local copies, waits for them, and re-layouts: none -> 1.26 us
where the time goes in v4:
time: 73.4 us; the launch traced here: 73.3 us
  Pallas kernels  71.4 us (97%)
  local copies, waits for them, and re-layouts  1.26 us (2%)
    pallas_call x1, Pallas kernels, body(): pl.pallas_call(kernel, out_shape=(field, field), in_specs=[hbm] * 8, out_...  71.4 us

profile of v4, /device:TPU:1, one launch (start us, length us, event | category | flops | bytes accessed | tf_op | source)
XLA Modules:
  0.0 73.3 jit_solution(2978461355507143890)
XLA Ops:
  0.6 71.4 %schwarz.1 = (f32[32,512]{1,0:T(8,128)S(1)}, f32[32,512]{1,0:T(8,128)S(1)}) custom-call(f32[32,512]{1,0:T(8,128)} %rhs_hbm.1, f32[1024,1024]{1,0:T(8,128)} %bitcast.6, f32[64,1024]{1,0:T(8,128)} %bitcast.9, f32[256,4096]{1,0:T(8,128)} %coarse_hbm.1, f32[1,1024]{1,0:T(1,128)} %bitcast.10, s32[80,1024]{1,0:T(8,128)} %bitcast.7, f32[80,1024]{1,0:T(8,128)} %bitcast.8, ...), custom_call_target="tpu_custom_call" | custom-call | tf_op jit(solution)/shard_map/schwarz/pallas_call | solution.py:563
  72.0 0.6 copy.12
  72.6 0.6 copy.13

commit v5 on v4

--- a/solution.py
+++ b/solution.py
@@ -203,7 +203,7 @@
         mine = slot_at(gy, gz)
         block = jnp.where(left, restricted[:16], restricted[16:])
         gathered[k, pl.ds(mine, 1)] = block.reshape(1, 16, 128)
-        for d in (4, 3, 5, 2, 6, 1, 7, 0):
+        for d in (0, 1, 7, 2, 6, 3, 5, 4):
             for flip in (1, 0):
                 if flip or d:
                     plane_copy(k, flip, d, mine).start()
@@ -416,7 +416,7 @@
     rhs = rhs_ref[...]
     halo_stage(0, pick(rhs))
     stiff_prepare()
-    stiff_build(0, 4)
+    stiff_build(0, 2)
     pl.semaphore_wait(barrier, len(greet))
     halo_send_all(0, 0)
     loads[2].wait()
@@ -438,13 +438,13 @@
             row = jnp.broadcast_to(sends_ref[f : f + 1, :], (128, 128))
             hit = jnp.broadcast_to(column, (128, 128)) == row
             gram[at, f * 128 : f * 128 + 128] = jnp.where(hit, 1.0, 0.0).astype(BF)
-    stiff_build(4, 8)
+    stiff_build(2, 7)
     restricted = restrict(rhs, own_cols)
     rim = halo_wait(0, 0)
     def stiff_step(t):
-        @pl.when(t == 1)
+        @pl.when(t < 3)
         def _():
-            at = 7 + t
+            at = 6 + t
             stiff_build(at, at)
 
     gather_start(0, restricted + restrict(rim, rim_cols))

time: 73.4 us -> 71.2 us (0.970)
  Pallas kernels: 71.4 us -> 69.2 us
    pallas_call x1, Pallas kernels: 71.4 us -> 69.2 us  [body(): pl.pallas_call(kernel, out_shape=(field, field), in_specs=[hbm] * 8, out_...]
where the time goes in v5:
time: 71.2 us; the launch traced here: 71.1 us
  Pallas kernels  69.2 us (97%)
  local copies, waits for them, and re-layouts  1.26 us (2%)
    pallas_call x1, Pallas kernels, body(): pl.pallas_call(kernel, out_shape=(field, field), in_specs=[hbm] * 8, out_...  69.2 us

profile of v5, /device:TPU:1, one launch (start us, length us, event | category | flops | bytes accessed | tf_op | source)
XLA Modules:
  0.0 71.1 jit_solution(7544013188684585205)
XLA Ops:
  0.6 69.2 %schwarz.1 = (f32[32,512]{1,0:T(8,128)S(1)}, f32[32,512]{1,0:T(8,128)S(1)}) custom-call(f32[32,512]{1,0:T(8,128)} %rhs_hbm.1, f32[1024,1024]{1,0:T(8,128)} %bitcast.6, f32[64,1024]{1,0:T(8,128)} %bitcast.9, f32[256,4096]{1,0:T(8,128)} %coarse_hbm.1, f32[1,1024]{1,0:T(1,128)} %bitcast.10, s32[80,1024]{1,0:T(8,128)} %bitcast.7, f32[80,1024]{1,0:T(8,128)} %bitcast.8, ...), custom_call_target="tpu_custom_call" | custom-call | tf_op jit(solution)/shard_map/schwarz/pallas_call | solution.py:563
  69.8 0.6 copy.12
  70.5 0.6 copy.13

commit v6 on v5

--- a/solution.py
+++ b/solution.py
@@ -100,7 +100,7 @@
     barrier = pltpu.get_barrier_semaphore()
     greet = [plane_peer(flip, d) for d in (4, 3, 5, 2, 6, 1, 7, 0) for flip in (1, 0) if flip or d]
     greet = greet + [x_peer(d) for d in (2, 1, 3)] + [(i, lax.rem(j + d, 4)) for d in (2, 1, 3)]
-    greet = greet + [(lax.rem(i + way, 64), lax.rem(j + d, 4)) for way in (1, 63) for d in range(4)]
+    greet = greet + beside[:2]
     for peer in greet:
         pl.semaphore_signal(barrier, inc=1, device_id=peer, device_id_type=pl.DeviceIdType.MESH)
 
@@ -455,9 +455,9 @@
     loads[7].wait()
     split_into(coarse_raw, coarse_hi, coarse_lo, 256, 32)
     fold_basis()
-    coarse_apply(0)
     local_finish(1)
     lent_buf[...] = pick(own_buf[...])
+    coarse_apply(0)
     stiff_build(9, 12)
     stiff_finish()
     spread = coarse_finish(0)

time: 71.2 us -> 70.4 us (0.989)
  Pallas kernels: 69.2 us -> 68.4 us
    pallas_call x1, Pallas kernels: 69.2 us -> 68.4 us  [body(): pl.pallas_call(kernel, out_shape=(field, field), in_specs=[hbm] * 8, out_...]
where the time goes in v6:
time: 70.4 us; the launch traced here: 70.3 us
  Pallas kernels  68.4 us (97%)
  local copies, waits for them, and re-layouts  1.26 us (2%)
    pallas_call x1, Pallas kernels, body(): pl.pallas_call(kernel, out_shape=(field, field), in_specs=[hbm] * 8, out_...  68.4 us

profile of v6, /device:TPU:1, one launch (start us, length us, event | category | flops | bytes accessed | tf_op | source)
XLA Modules:
  0.0 70.3 jit_solution(17249097091679006441)
XLA Ops:
  0.6 68.4 %schwarz.1 = (f32[32,512]{1,0:T(8,128)S(1)}, f32[32,512]{1,0:T(8,128)S(1)}) custom-call(f32[32,512]{1,0:T(8,128)} %rhs_hbm.1, f32[1024,1024]{1,0:T(8,128)} %bitcast.6, f32[64,1024]{1,0:T(8,128)} %bitcast.9, f32[256,4096]{1,0:T(8,128)} %coarse_hbm.1, f32[1,1024]{1,0:T(1,128)} %bitcast.10, s32[80,1024]{1,0:T(8,128)} %bitcast.7, f32[80,1024]{1,0:T(8,128)} %bitcast.8, ...), custom_call_target="tpu_custom_call" | custom-call | tf_op jit(solution)/shard_map/schwarz/pallas_call | solution.py:563
  69.1 0.6 copy.12
  69.7 0.6 copy.13
